TPU v7x, 128 devices: a whole 4x4x4 slice. The times are simulated.
128 devices in a mesh: pipe: 2 (over x_lo), dp: 32 (over x_hi, z, y), tensor: 2 (over core).
Axes of the slice: x: 4 (x_hi: 2, x_lo: 2; x = x_hi * 2 + x_lo), y: 4, z: 4, core: 2. Of those that a mesh axis runs over, the one named last changes fastest.
Arguments:
- inputs: bfloat16 [2, 4096, 896], P(None, ('dp', 'tensor')), may hold values from -16 to 16
- cotangent: bfloat16 [2, 4096, 896], P(None, ('dp', 'tensor')), may hold values from -16 to 16
- lengths: int32 [2, 32, 4], P(None, 'dp'), may hold values from 0 to 128, as said below
- gain_attn: bfloat16 [2, 896], P('pipe'), may hold values from 0.099609375 to 1.8984375
- w_query: bfloat16 [2, 896, 896], P('pipe', None, 'tensor'), may hold values from -0.1875 to 0.1875
- b_query: bfloat16 [2, 896], P('pipe', 'tensor'), may hold values from -3 to 3
- w_keyval: bfloat16 [2, 896, 2, 128], P('pipe', None, 'tensor'), may hold values from -0.1875 to 0.1875
- b_keyval: bfloat16 [2, 2, 128], P('pipe', 'tensor'), may hold values from -3 to 3
- w_out: bfloat16 [2, 896, 896], P('pipe', 'tensor'), may hold values from -0.75 to 0.75
- gain_mlp: bfloat16 [2, 896], P('pipe'), may hold values from 0.099609375 to 1.8984375
- w_gate_up: bfloat16 [2, 896, 2, 4864], P('pipe', None, None, 'tensor'), may hold values from -0.1875 to 0.1875
- w_down: bfloat16 [2, 4864, 896], P('pipe', 'tensor'), may hold values from -0.078125 to 0.078125
Outputs:
- section_out: bfloat16 [2, 2, 4096, 896], P('pipe', None, ('dp', 'tensor'))
- input_grad: float32 [2, 2, 4096, 896], P('pipe', None, ('dp', 'tensor'))
- grad_gain_attn: float32 [2, 896], P('pipe')
- grad_w_query: float32 [2, 896, 896], P('pipe', 'dp', 'tensor')
- grad_b_query: float32 [2, 896], P('pipe')
- grad_w_keyval: float32 [2, 896, 2, 128], P('pipe', 'dp', 'tensor')
- grad_b_keyval: float32 [2, 2, 128], P('pipe')
- grad_w_out: float32 [2, 896, 896], P('pipe', 'tensor', 'dp')
- grad_gain_mlp: float32 [2, 896], P('pipe')
- grad_w_gate_up: float32 [2, 896, 2, 4864], P('pipe', 'dp', None, 'tensor')
- grad_w_down: float32 [2, 4864, 896], P('pipe', 'tensor', 'dp')
Inputs may be any that keep to these rules, and one draw needn't show every extreme that they name: In every micro-batch the lengths of one rank sum to more than 64 and at most 128; each rank's first sequence is longer than 64; in every micro-batch some rank holds a single sequence of exactly 128; later lengths may be 0.
All inputs are finite; a program needn't handle non-finite values.
Results may differ from a plain program's by a relative error of at most 0.03.
Values may be sent and summed in bfloat16 or wider, within the bound.
A program may use at most 256 MiB of HBM per device.

v0:
```python
import jax
import jax.numpy as jnp
from jax import lax
from jax.sharding import PartitionSpec as P

D = 896
HEADS = 14
KV_HEADS = 2
HEAD = 64
CAP = 128
SEQS = 4


EPS = 1e-06
THETA = 1000000.0


def laid_out(tiles, dim):
    shape = list(tiles.shape[1:])
    shape[dim] *= tiles.shape[0]
    return jnp.moveaxis(tiles, 0, dim).reshape(shape)


def copy_for_each(shard, axis):
    peers = lax.axis_size(axis)
    return lax.all_to_all(
        jnp.broadcast_to(shard[None], (peers, *shard.shape)), axis, 0, 0, tiled=True
    )


def collect(shard, axis, dim):
    return laid_out(copy_for_each(shard, axis), dim)


def cut_along(shard, dim, peers):
    before, after = (shard.shape[:dim], shard.shape[dim + 1 :])
    return jnp.moveaxis(shard.reshape(*before, peers, -1, *after), dim, 0)


def sent_and_summed(shard, axis, dim):
    tiles = cut_along(shard, dim, lax.axis_size(axis))
    arrived = lax.all_to_all(tiles, axis, split_axis=0, concat_axis=0, tiled=True)
    return arrived.astype(jnp.float32).sum(axis=0)


def passed_along(shard, axis, by):
    peers = lax.axis_size(axis)
    pairs = [(i, i + by) for i in range(peers) if 0 <= i + by < peers]
    return lax.ppermute(shard, axis, pairs)


def taken_together(shard, axis):
    everything = copy_for_each(shard, axis)
    return jnp.sum(everything, axis=0)


def in_one(arrays, axis):
    ends = [0]
    for a in arrays:
        ends.append(ends[-1] + a.size)
    total = taken_together(jnp.concatenate([a.ravel() for a in arrays]), axis)
    return tuple((total[b:e].reshape(a.shape) for a, b, e in zip(arrays, ends, ends[1:])))


def layout(rank_lengths):
    seq_ends = jnp.cumsum(rank_lengths)
    seq_starts = seq_ends - rank_lengths
    slot_index = jnp.arange(CAP, dtype=jnp.int32)
    segment = jnp.sum((slot_index[:, None] >= seq_ends[None, :]).astype(jnp.int32), axis=1)
    starts_all = jnp.concatenate([seq_starts, seq_ends[-1:]])
    one_hot = (segment[:, None] == jnp.arange(SEQS + 1, dtype=jnp.int32)[None, :]).astype(jnp.int32)
    slot_start = jnp.sum(one_hot * starts_all[None, :], axis=1)
    return (segment, slot_index - slot_start)


def rotary_angles(position):
    half_width = HEAD // 2
    frequency = THETA ** (-(jnp.arange(half_width, dtype=jnp.float32) * 2.0 / HEAD))
    phases = position.astype(jnp.float32)[:, None] * frequency[None, :]
    phases = jnp.concatenate([phases, phases], axis=1)
    return (jnp.cos(phases)[:, None, :], jnp.sin(phases)[:, None, :])


def rotate(values, cosine_table, sine_table):
    half_width = values.shape[-1] // 2
    turned = jnp.concatenate([-values[..., half_width:], values[..., :half_width]], axis=-1)
    return values * cosine_table + turned * sine_table


def visible(segment):
    slot_index = jnp.arange(segment.shape[0], dtype=jnp.int32)
    return (segment[:, None] == segment[None, :]) & (slot_index[None, :] <= slot_index[:, None])


def raw_scores(queries, key_heads, allowed):
    scores = jnp.einsum(
        "igkd,jgd->gkij", queries, key_heads, preferred_element_type=jnp.float32
    ) * HEAD ** (-0.5)
    return jnp.where(allowed, scores, -1e30)


def gather_rows(values):
    return collect(values, "tensor", 0)


def sum_rows(values):
    return sent_and_summed(values.astype(jnp.bfloat16), "tensor", 0)


def gather_grads(values):
    return collect(values, "tensor", 0)


def sum_grads(values):
    return sent_and_summed(values.astype(jnp.bfloat16), "tensor", 0)


def norm_back(grad_normed, values, inverse, gain):
    scaled = values * inverse
    gain_term = jnp.sum(grad_normed * scaled, axis=0)
    weighted = grad_normed * gain
    grad_values = inverse * (
        weighted - scaled * jnp.mean(weighted * scaled, axis=-1, keepdims=True)
    )
    return (grad_values, gain_term)


def forward(stream, params, segment, position):
    gain_one, w_q, b_q, w_kv, b_kv, w_o, gain_two, w_gu, w_d = params
    row_count = segment.shape[0]
    per_group = HEADS // KV_HEADS
    inverse_one = lax.rsqrt(jnp.mean(stream * stream, axis=-1, keepdims=True) + EPS)
    normed = gather_rows((stream * inverse_one * gain_one).astype(jnp.bfloat16))
    cosine_table, sine_table = rotary_angles(position)
    queries = jnp.dot(normed, w_q, preferred_element_type=jnp.float32) + b_q
    keyval = jnp.einsum("id,dge->ige", normed, w_kv, preferred_element_type=jnp.float32) + b_kv
    group_count = keyval.shape[1]
    queries = rotate(
        queries.reshape(row_count, group_count * per_group, HEAD), cosine_table, sine_table
    )
    queries = queries.astype(jnp.bfloat16).reshape(row_count, group_count, per_group, HEAD)
    key_heads = rotate(keyval[..., :HEAD], cosine_table, sine_table).astype(jnp.bfloat16)
    values = keyval[..., HEAD:].astype(jnp.bfloat16)
    scores = raw_scores(queries, key_heads, visible(segment))
    row_top = jnp.max(scores, axis=-1, keepdims=True)
    logsum = row_top + jnp.log(jnp.sum(jnp.exp(scores - row_top), axis=-1, keepdims=True))
    soft_weights = jnp.exp(scores - logsum).astype(jnp.bfloat16)
    mixture = jnp.einsum("gkij,jgd->igkd", soft_weights, values, preferred_element_type=jnp.float32)
    mixture = mixture.reshape(row_count, group_count * per_group * HEAD).astype(jnp.bfloat16)
    middle = stream + sum_rows(jnp.dot(mixture, w_o, preferred_element_type=jnp.float32))
    inverse_two = lax.rsqrt(jnp.mean(middle * middle, axis=-1, keepdims=True) + EPS)
    normed_two = gather_rows((middle * inverse_two * gain_two).astype(jnp.bfloat16))
    gate_up = jnp.einsum("id,dgf->igf", normed_two, w_gu, preferred_element_type=jnp.float32)
    hidden = (jax.nn.silu(gate_up[:, 0]) * gate_up[:, 1]).astype(jnp.bfloat16)
    result = middle + sum_rows(jnp.dot(hidden, w_d, preferred_element_type=jnp.float32))
    return (
        result,
        (
            stream,
            inverse_one,
            normed,
            queries,
            key_heads,
            values,
            logsum,
            mixture,
            middle,
            inverse_two,
            normed_two,
            gate_up,
            hidden,
        ),
    )


def backward(upstream, saved_state, params, segment, position):
    gain_one, w_q, b_q, w_kv, b_kv, w_o, gain_two, w_gu, w_d = params
    (
        stream,
        inverse_one,
        normed,
        queries,
        key_heads,
        values,
        logsum,
        mixture,
        middle,
        inverse_two,
        normed_two,
        gate_up,
        hidden,
    ) = saved_state
    row_count, group_count, per_group, head_width = queries.shape
    branch = gather_grads(upstream.astype(jnp.bfloat16))
    g_down = jnp.einsum("if,id->fd", hidden, branch, preferred_element_type=jnp.float32)
    grad_hidden = jnp.einsum("id,fd->if", branch, w_d, preferred_element_type=jnp.float32)
    gate_part = gate_up[:, 0]
    up_part = gate_up[:, 1]
    sigmoid_gate = jax.nn.sigmoid(gate_part)
    grad_gate = grad_hidden * up_part * sigmoid_gate * (1.0 + gate_part * (1.0 - sigmoid_gate))
    grad_up = grad_hidden * gate_part * sigmoid_gate
    grad_gate_up = jnp.stack([grad_gate, grad_up], axis=1).astype(jnp.bfloat16)
    g_gate_up = jnp.einsum(
        "id,igf->dgf", normed_two, grad_gate_up, preferred_element_type=jnp.float32
    )
    grad_normed = sum_grads(
        jnp.einsum("igf,dgf->id", grad_gate_up, w_gu, preferred_element_type=jnp.float32)
    )
    grad_middle, g_gain_two = norm_back(grad_normed, middle, inverse_two, gain_two)
    grad_middle = grad_middle + upstream
    branch = gather_grads(grad_middle.astype(jnp.bfloat16))
    g_out = jnp.einsum("ie,id->ed", mixture, branch, preferred_element_type=jnp.float32)
    grad_mixture = jnp.einsum("id,ed->ie", branch, w_o, preferred_element_type=jnp.float32)
    grad_mixture = grad_mixture.astype(jnp.bfloat16).reshape(
        row_count, group_count, per_group, head_width
    )
    soft_weights = jnp.exp(raw_scores(queries, key_heads, visible(segment)) - logsum)
    grad_values = jnp.einsum(
        "gkij,igkd->jgd",
        soft_weights.astype(jnp.bfloat16),
        grad_mixture,
        preferred_element_type=jnp.float32,
    )
    grad_soft = jnp.einsum(
        "igkd,jgd->gkij", grad_mixture, values, preferred_element_type=jnp.float32
    )
    grad_scores = soft_weights * (
        grad_soft - jnp.sum(soft_weights * grad_soft, axis=-1, keepdims=True)
    )
    grad_scores = grad_scores.astype(jnp.bfloat16)
    scaling = HEAD ** (-0.5)
    grad_queries = (
        jnp.einsum("gkij,jgd->igkd", grad_scores, key_heads, preferred_element_type=jnp.float32)
        * scaling
    )
    grad_keys = (
        jnp.einsum("gkij,igkd->jgd", grad_scores, queries, preferred_element_type=jnp.float32)
        * scaling
    )
    cosine_table, sine_table = rotary_angles(position)
    grad_query = rotate(
        grad_queries.reshape(row_count, group_count * per_group, head_width),
        cosine_table,
        -sine_table,
    )
    grad_query = grad_query.reshape(row_count, group_count * per_group * head_width).astype(
        jnp.bfloat16
    )
    grad_keyval = jnp.concatenate(
        [rotate(grad_keys, cosine_table, -sine_table), grad_values], axis=-1
    ).astype(jnp.bfloat16)
    g_query = jnp.einsum("id,ie->de", normed, grad_query, preferred_element_type=jnp.float32)
    g_keyval = jnp.einsum("id,ige->dge", normed, grad_keyval, preferred_element_type=jnp.float32)
    g_bias_query = jnp.sum(grad_query.astype(jnp.float32), axis=0)
    g_bias_keyval = jnp.sum(grad_keyval.astype(jnp.float32), axis=0)
    grad_normed = jnp.einsum("ie,de->id", grad_query, w_q, preferred_element_type=jnp.float32)
    grad_normed = grad_normed + jnp.einsum(
        "ige,dge->id", grad_keyval, w_kv, preferred_element_type=jnp.float32
    )
    grad_normed = sum_grads(grad_normed)
    grad_stream, g_gain_one = norm_back(grad_normed, stream, inverse_one, gain_one)
    grad_stream = grad_stream + grad_middle
    large_terms = (g_query, g_keyval, g_out, g_gate_up, g_down)
    small_terms = (g_gain_one, g_gain_two, g_bias_query, g_bias_keyval)
    return (grad_stream, large_terms, small_terms)


def body(
    inputs,
    cotangent,
    lengths,
    gain_attn,
    w_query,
    b_query,
    w_keyval,
    b_keyval,
    w_out,
    gain_mlp,
    w_gate_up,
    w_down,
):
    section_index = lax.axis_index("pipe")
    first_section = section_index == 0
    params = (
        gain_attn[0].astype(jnp.float32),
        w_query[0],
        b_query[0].astype(jnp.float32),
        w_keyval[0],
        b_keyval[0].astype(jnp.float32),
        w_out[0],
        gain_mlp[0].astype(jnp.float32),
        w_gate_up[0],
        w_down[0],
    )
    micro_count = inputs.shape[0]
    local_rows = inputs.shape[1]
    tensor_index = lax.axis_index("tensor")
    segments = []
    positions = []
    for micro_slot in range(micro_count):
        segment, position = layout(lengths[micro_slot, 0])
        segments.append(segment)
        positions.append(position)
    segments = jnp.stack(segments)
    positions = jnp.stack(positions)

    def select_micro(table, micro_index):
        return lax.dynamic_index_in_dim(
            table, jnp.clip(micro_index, 0, micro_count - 1), 0, keepdims=False
        )

    received = jnp.zeros((local_rows, D), jnp.float32)
    outputs = []
    stored = []
    for step_index in range(micro_count + 1):
        micro_index = step_index - section_index
        stream = jnp.where(
            first_section, inputs[min(step_index, micro_count - 1)].astype(jnp.float32), received
        )
        result, saved_state = forward(
            stream,
            params,
            select_micro(segments, micro_index),
            select_micro(positions, micro_index),
        )
        result = result.astype(jnp.bfloat16)
        outputs.append(result)
        stored.append(saved_state)
        if step_index < micro_count:
            received = passed_along(result, "pipe", 1).astype(jnp.float32)
    section_out = jnp.stack(
        [
            jnp.where(first_section, outputs[micro_slot], outputs[micro_slot + 1])
            for micro_slot in range(micro_count)
        ]
    )
    received = jnp.zeros((local_rows, D), jnp.float32)
    returned = []
    totals = None
    shares = None
    small_sums = None
    for step_index in range(micro_count + 1):
        micro_index = step_index + section_index - 1
        segment = select_micro(segments, micro_index)
        position = select_micro(positions, micro_index)
        own_segment = lax.dynamic_slice_in_dim(segment, tensor_index * local_rows, local_rows)
        live_rows = (own_segment < SEQS).astype(jnp.float32)[:, None]
        in_range = (micro_index < micro_count).astype(jnp.float32)
        supplied = select_micro(cotangent, micro_index).astype(jnp.float32) * live_rows * in_range
        upstream = jnp.where(first_section, received, supplied)
        earlier = stored[max(step_index - 1, 0)]
        following = stored[min(step_index + 1, micro_count)]
        chosen = jax.tree.map(lambda a, b: jnp.where(first_section, a, b), earlier, following)
        saved_state = chosen
        grad_stream, large_terms, small_terms = backward(
            upstream, saved_state, params, segment, position
        )
        returned.append(grad_stream)
        if step_index < micro_count:
            received = passed_along(grad_stream.astype(jnp.bfloat16), "pipe", -1).astype(
                jnp.float32
            )
        small_sums = (
            small_terms if small_sums is None else jax.tree.map(jnp.add, small_sums, small_terms)
        )
        totals = large_terms if totals is None else jax.tree.map(jnp.add, totals, large_terms)
    shares = (
        lax.psum_scatter(
            totals[0].astype(jnp.bfloat16), "dp", scatter_dimension=0, tiled=True
        ).astype(jnp.float32),
        lax.psum_scatter(
            totals[1].astype(jnp.bfloat16), "dp", scatter_dimension=0, tiled=True
        ).astype(jnp.float32),
        lax.psum_scatter(
            totals[2].astype(jnp.bfloat16), "dp", scatter_dimension=1, tiled=True
        ).astype(jnp.float32),
        lax.psum_scatter(
            totals[3].astype(jnp.bfloat16), "dp", scatter_dimension=0, tiled=True
        ).astype(jnp.float32),
        lax.psum_scatter(
            totals[4].astype(jnp.bfloat16), "dp", scatter_dimension=1, tiled=True
        ).astype(jnp.float32),
    )
    input_grad = jnp.stack(
        [
            jnp.where(first_section, returned[micro_slot + 1], returned[micro_slot])
            for micro_slot in range(micro_count)
        ]
    )
    g_gain_one, g_gain_two, g_bias_query, g_bias_keyval = small_sums
    query_width = g_bias_query.shape[0]
    group_count = g_bias_keyval.shape[0]
    full_query = lax.dynamic_update_slice(
        jnp.zeros((HEADS * HEAD,), jnp.float32), g_bias_query, (tensor_index * query_width,)
    )
    full_keyval = lax.dynamic_update_slice(
        jnp.zeros((KV_HEADS, 2 * HEAD), jnp.float32), g_bias_keyval, (tensor_index * group_count, 0)
    )
    gain_one_total, gain_two_total, query_total, keyval_total = in_one(
        (g_gain_one, g_gain_two, full_query, full_keyval), ("dp", "tensor")
    )
    g_query, g_keyval, g_out, g_gate_up, g_down = shares
    return (
        section_out[None],
        input_grad[None],
        gain_one_total[None],
        g_query[None],
        query_total[None],
        g_keyval[None],
        keyval_total[None],
        g_out[None],
        gain_two_total[None],
        g_gate_up[None],
        g_down[None],
    )


def solution(mesh):
    placed = (
        P(None, ("dp", "tensor"), None),
        P(None, ("dp", "tensor"), None),
        P(None, "dp", None),
        P("pipe", None),
        P("pipe", None, "tensor"),
        P("pipe", "tensor"),
        P("pipe", None, "tensor", None),
        P("pipe", "tensor", None),
        P("pipe", "tensor", None),
        P("pipe", None),
        P("pipe", None, None, "tensor"),
        P("pipe", "tensor", None),
    )
    return jax.shard_map(
        body,
        mesh=mesh,
        in_specs=placed,
        out_specs=(
            P("pipe", None, ("dp", "tensor"), None),
            P("pipe", None, ("dp", "tensor"), None),
            P("pipe", None),
            P("pipe", "dp", "tensor"),
            P("pipe", None),
            P("pipe", "dp", "tensor", None),
            P("pipe", None, None),
            P("pipe", "tensor", "dp"),
            P("pipe", None),
            P("pipe", "dp", None, "tensor"),
            P("pipe", "tensor", "dp"),
        ),
        check_vma=False,
    )
```

profile of v0, /device:TPU:0, one launch (start us, length us, event | category | flops | bytes accessed | tf_op | source)
XLA Modules:
  0.0 733.4 jit_solution(4682669029444329560)
XLA Ops:
  33.1 4.2 all_to_all.126
  37.2 5.0 fusion.26
  90.7 6.6 broadcast_select_fusion.2
  98.9 4.6 all_to_all.131
  104.2 4.3 all-to-all-start.12
  111.3 6.4 fusion.125
  170.9 5.1 broadcast_select_fusion
  187.2 8.5 %fusion.106 = f32[896,2,2432]{2,0,1:T(8,128)} fusion(bf16[128,1,2432]{2,0,1:T(8,128)(2,1)S(1)} %copy-done.85, bf16[128,1,2432]{2,0,1:T(8,128)(2,1)S(1)} %copy-done.83, bf16[128,896]{1,0:T(8,128)(2,1)S(1)} %get-tuple-element.125), kind=kOutput, calls=%fused_computation.147 | convolution fusion | flops 1118175232 | bytes 18907136 | tf_op jit(solution)/shard_map/id,igf->dgf/dot_general | solution.py:203
  200.5 5.6 fusion.123
  215.3 4.3 all_to_all.140
  235.0 8.4 %fusion.105 = f32[896,2,2432]{2,0,1:T(8,128)} fusion(bf16[128,1,2432]{2,0,1:T(8,128)(2,1)S(1)} %get-tuple-element.118, bf16[128,1,2432]{2,0,1:T(8,128)(2,1)S(1)} %get-tuple-element.117, bf16[128,896]{1,0:T(8,128)(2,1)S(1)} %get-tuple-element.126), kind=kOutput, calls=%fused_computation.146 | convolution fusion | flops 1118175232 | bytes 18907136 | tf_op jit(solution)/shard_map/id,igf->dgf/dot_general | solution.py:203
  258.3 16.2 %add_convert_fusion = bf16[896,2,2432]{2,0,1:T(8,128)(2,1)} fusion(f32[896,2,2432]{2,0,1:T(8,128)} %fusion.106, f32[896,2,2432]{2,0,1:T(8,128)} %fusion.105, bf16[128,1,2432]{2,0,1:T(8,128)(2,1)} %copy-done.81, bf16[128,1,2432]{2,0,1:T(8,128)(2,1)} %copy-done.80, bf16[128,896]{1,0:T(8,128)(2,1)S(1)} %get-tuple-element.124), kind=kOutput, calls=%fused_computation | convolution fusion | flops 1131249664 | bytes 45056000 | tf_op jit(solution)/shard_map/id,igf->dgf/dot_general | solution.py:203
  274.5 34.4 %copy.123 = bf16[896,2,2432]{2,1,0:T(2,128)(2,1)} copy(bf16[896,2,2432]{2,0,1:T(8,128)(2,1)} %add_convert_fusion) | data formatting | bytes 17432576 | tf_op jit(solution)/shard_map/convert_element_type | solution.py:378
  322.1 6.9 add_convert_fusion.1
  329.1 156.6 %fusion.346 = (bf16[32,448]{1,0:T(8,128)(2,1)}, bf16[32,128]{1,0:T(8,128)(2,1)}, bf16[448,32]{0,1:T(8,128)(2,1)S(1)}, bf16[2432,32]{0,1:T(8,128)(2,1)}) fusion(bf16[896,448]{1,0:T(8,128)(2,1)} %add_convert_fusion.3, bf16[896,1,128]{2,0,1:T(8,128)(2,1)} %fusion.92, bf16[448,896]{0,1:T(8,128)(2,1)S(1)} %add_convert_fusion.2, ...), kind=kCustom, calls=%all-reduce-scatter.4 | all-reduce-scatter fusion | flops 3538945 | bytes 6414848
  489.1 5.1 collective-permute-start.8
  504.0 15.9 %all-to-all-start.24 = ((f32[64,1,2944]{2,1,0:T(1,128)}), f32[64,1,2944]{2,1,0:T(1,128)S(1)}, u32[]{:S(2)}, u32[]{:S(2)}) async-start(f32[64,1,2944]{2,1,0:T(1,128)} %broadcast_in_dim.125), calls=%async_computation.24 | async-start | bytes 1507328 | tf_op jit(solution)/shard_map/all_to_all | solution.py:26
  524.5 4.6 collective-permute-start.6
  539.6 6.7 collective-permute-start.14
  551.2 6.5 collective-permute-start.15
  561.4 5.3 collective-permute-start.18
  572.9 14.2 %collective-permute-start.19 = (bf16[2432,28]{0,1:T(8,128)(2,1)S(1)}, bf16[2432,28]{0,1:T(8,128)(2,1)S(1)}, u32[]{:S(2)}, u32[]{:S(2)}) collective-permute-start(bf16[2432,28]{0,1:T(8,128)(2,1)S(1)} %slice.275), channel_id=1, source_target_pairs={{0,8},{2,10},{4,12},{6,14},{8,16},{10,18},{12,20},{14,22},{16,24},... | collective-permute-start | bytes 408584
  589.2 9.9 %collective-permute-done.19 = bf16[2432,28]{0,1:T(8,128)(2,1)S(1)} collective-permute-done((bf16[2432,28]{0,1:T(8,128)(2,1)S(1)}, bf16[2432,28]{0,1:T(8,128)(2,1)S(1)}, u32[]{:S(2)}, u32[]{:S(2)}) %collective-permute-start.19) | collective-permute-done | bytes 136224
  605.9 118.4 %all-reduce.12.cloned.1.call-done = bf16[896,2,2432]{2,1,0:T(2,128)(2,1)} async-done(((bf16[896,2,2432]{2,1,0:T(2,128)(2,1)}), bf16[896,2,2432]{2,1,0:T(2,128)(2,1)}) %all-reduce.12.cloned.1.call-update) | async-done | bytes 8716304
  (674 shorter events, 250.9 us)
Async XLA Ops:
  11.3 9.7 %all-to-all-start = ((bf16[2,64,896]{2,1,0:T(8,128)(2,1)}), bf16[2,64,896]{2,1,0:T(8,128)(2,1)S(1)}, u32[]{:S(2)}, u32[]{:S(2)}) async-start(bf16[2,64,896]{2,1,0:T(8,128)(2,1)} %broadcast_in_dim.100), calls=%async_computation | async-start | bytes 458752 | tf_op jit(solution)/shard_map/all_to_all | solution.py:26
  48.2 20.1 %collective-permute-start = (bf16[64,896]{1,0:T(8,128)(2,1)}, bf16[64,896]{1,0:T(8,128)(2,1)}, u32[]{:S(2)}, u32[]{:S(2)}) collective-permute-start(bf16[64,896]{1,0:T(8,128)(2,1)} %add_convert_fusion.9), channel_id=1, source_target_pairs={{0,64},{1,65},{2,66},{3,67},{4,68},{5,69},{6,70},{7,71},{8,72},{9,... | collective-permute-start | bytes 344072 | tf_op jit(solution)/shard_map/ppermute | solution.py:49
  104.2 7.0 all-to-all-start.12
  140.1 7.5 %all-to-all-start.15 = ((bf16[2,64,896]{2,1,0:T(8,128)(2,1)}), bf16[2,64,896]{2,1,0:T(8,128)(2,1)}, u32[]{:S(2)}, u32[]{:S(2)}) async-start(bf16[2,64,896]{2,1,0:T(8,128)(2,1)} %bitcast.894), calls=%async_computation.15 | async-start | bytes 458752 | tf_op jit(solution)/shard_map/all_to_all | solution.py:42
  144.2 580.2 %all-reduce.12.cloned.1.call-start = ((), (), s32[]{:S(2)}) async-start(), calls=%async_computation.25 | async-start | bytes 17432576
  181.4 15.0 %collective-permute-start.2 = (bf16[64,896]{1,0:T(8,128)(2,1)S(1)}, bf16[64,896]{1,0:T(8,128)(2,1)S(1)}, u32[]{:S(2)}, u32[]{:S(2)}) collective-permute-start(bf16[64,896]{1,0:T(8,128)(2,1)S(1)} %get-tuple-element.96), channel_id=1, source_target_pairs={{64,0},{65,1},{66,2},{67,3},{68,4},{69,5},{70,6},{71,7},{72,8},{73... | collective-permute-start | bytes 344072 | tf_op jit(solution)/shard_map/ppermute | solution.py:49
  230.3 14.8 %collective-permute-start.3 = (bf16[64,896]{1,0:T(8,128)(2,1)S(1)}, bf16[64,896]{1,0:T(8,128)(2,1)S(1)}, u32[]{:S(2)}, u32[]{:S(2)}) collective-permute-start(bf16[64,896]{1,0:T(8,128)(2,1)S(1)} %convert_element_type.694), channel_id=1, source_target_pairs={{64,0},{65,1},{66,2},{67,3},{68,4},{69,5},{70,6},{71,7},{72,8},{73... | collective-permute-start | bytes 344072 | tf_op jit(solution)/shard_map/ppermute | solution.py:49
  486.5 46.9 %collective-permute-start.10 = (bf16[32,128]{1,0:T(8,128)(2,1)}, bf16[32,128]{1,0:T(8,128)(2,1)S(1)}, u32[]{:S(2)}, u32[]{:S(2)}) collective-permute-start(bf16[32,128]{1,0:T(8,128)(2,1)} %get-tuple-element.73), channel_id=1, source_target_pairs={{0,6},{2,8},{4,10},{6,12},{8,14},{10,16},{12,18},{14,20},{16,22},{... | collective-permute-start | bytes 24584
  487.8 49.0 %collective-permute-start.9 = (bf16[32,128]{1,0:T(8,128)(2,1)}, bf16[32,128]{1,0:T(8,128)(2,1)S(1)}, u32[]{:S(2)}, u32[]{:S(2)}) collective-permute-start(bf16[32,128]{1,0:T(8,128)(2,1)} %get-tuple-element.73), channel_id=1, source_target_pairs={{0,4},{2,6},{4,8},{6,10},{8,12},{10,14},{12,16},{14,18},{16,20},{1... | collective-permute-start | bytes 24584
  489.1 50.5 %collective-permute-start.8 = (bf16[32,128]{1,0:T(8,128)(2,1)}, bf16[32,128]{1,0:T(8,128)(2,1)S(1)}, u32[]{:S(2)}, u32[]{:S(2)}) collective-permute-start(bf16[32,128]{1,0:T(8,128)(2,1)} %get-tuple-element.73), channel_id=1, source_target_pairs={{0,2},{2,4},{4,6},{6,8},{8,10},{10,12},{12,14},{14,16},{16,18},{18... | collective-permute-start | bytes 24584
  504.0 99.2 %all-to-all-start.24 = ((f32[64,1,2944]{2,1,0:T(1,128)}), f32[64,1,2944]{2,1,0:T(1,128)S(1)}, u32[]{:S(2)}, u32[]{:S(2)}) async-start(f32[64,1,2944]{2,1,0:T(1,128)} %broadcast_in_dim.125), calls=%async_computation.24 | async-start | bytes 1507328 | tf_op jit(solution)/shard_map/all_to_all | solution.py:26
  519.8 9.2 %collective-permute-start.11 = (bf16[28,128]{1,0:T(8,128)(2,1)S(1)}, bf16[28,128]{1,0:T(8,128)(2,1)S(1)}, u32[]{:S(2)}, u32[]{:S(2)}) collective-permute-start(bf16[28,128]{1,0:T(8,128)(2,1)S(1)} %slice.273), channel_id=1, source_target_pairs={{0,8},{2,10},{4,12},{6,14},{8,16},{10,18},{12,20},{14,22},{16,24},... | collective-permute-start | bytes 21512
  524.5 26.7 %collective-permute-start.6 = (bf16[32,448]{1,0:T(8,128)(2,1)S(1)}, bf16[32,448]{1,0:T(8,128)(2,1)S(1)}, u32[]{:S(2)}, u32[]{:S(2)}) collective-permute-start(bf16[32,448]{1,0:T(8,128)(2,1)S(1)} %copy-done.102), channel_id=1, source_target_pairs={{0,6},{2,8},{4,10},{6,12},{8,14},{10,16},{12,18},{14,20},{16,22},{... | collective-permute-start | bytes 86024
  529.1 18.5 %collective-permute-start.7 = (bf16[28,448]{1,0:T(8,128)(2,1)S(1)}, bf16[28,448]{1,0:T(8,128)(2,1)S(1)}, u32[]{:S(2)}, u32[]{:S(2)}) collective-permute-start(bf16[28,448]{1,0:T(8,128)(2,1)S(1)} %slice.272), channel_id=1, source_target_pairs={{0,8},{2,10},{4,12},{6,14},{8,16},{10,18},{12,20},{14,22},{16,24},... | collective-permute-start | bytes 75272
  533.4 24.9 %collective-permute-start.5 = (bf16[32,448]{1,0:T(8,128)(2,1)S(1)}, bf16[32,448]{1,0:T(8,128)(2,1)S(1)}, u32[]{:S(2)}, u32[]{:S(2)}) collective-permute-start(bf16[32,448]{1,0:T(8,128)(2,1)S(1)} %copy-done.102), channel_id=1, source_target_pairs={{0,4},{2,6},{4,8},{6,10},{8,12},{10,14},{12,16},{14,18},{16,20},{1... | collective-permute-start | bytes 86024
  536.8 24.6 %collective-permute-start.4 = (bf16[32,448]{1,0:T(8,128)(2,1)S(1)}, bf16[32,448]{1,0:T(8,128)(2,1)S(1)}, u32[]{:S(2)}, u32[]{:S(2)}) collective-permute-start(bf16[32,448]{1,0:T(8,128)(2,1)S(1)} %copy-done.102), channel_id=1, source_target_pairs={{0,2},{2,4},{4,6},{6,8},{8,10},{10,12},{12,14},{14,16},{16,18},{18... | collective-permute-start | bytes 86024
  539.6 30.6 %collective-permute-start.14 = (bf16[448,32]{0,1:T(8,128)(2,1)S(1)}, bf16[448,32]{0,1:T(8,128)(2,1)S(1)}, u32[]{:S(2)}, u32[]{:S(2)}) collective-permute-start(bf16[448,32]{0,1:T(8,128)(2,1)S(1)} %get-tuple-element.74), channel_id=1, source_target_pairs={{0,6},{2,8},{4,10},{6,12},{8,14},{10,16},{12,18},{14,20},{16,22},{... | collective-permute-start | bytes 86024
  547.6 25.4 %collective-permute-start.13 = (bf16[448,32]{0,1:T(8,128)(2,1)S(1)}, bf16[448,32]{0,1:T(8,128)(2,1)S(1)}, u32[]{:S(2)}, u32[]{:S(2)}) collective-permute-start(bf16[448,32]{0,1:T(8,128)(2,1)S(1)} %get-tuple-element.74), channel_id=1, source_target_pairs={{0,4},{2,6},{4,8},{6,10},{8,12},{10,14},{12,16},{14,18},{16,20},{1... | collective-permute-start | bytes 86024
  551.2 16.2 %collective-permute-start.15 = (bf16[448,28]{0,1:T(8,128)(2,1)S(1)}, bf16[448,28]{0,1:T(8,128)(2,1)S(1)}, u32[]{:S(2)}, u32[]{:S(2)}) collective-permute-start(bf16[448,28]{0,1:T(8,128)(2,1)S(1)} %slice.274), channel_id=1, source_target_pairs={{0,8},{2,10},{4,12},{6,14},{8,16},{10,18},{12,20},{14,22},{16,24},... | collective-permute-start | bytes 75272
  558.3 29.6 %collective-permute-start.12 = (bf16[448,32]{0,1:T(8,128)(2,1)S(1)}, bf16[448,32]{0,1:T(8,128)(2,1)S(1)}, u32[]{:S(2)}, u32[]{:S(2)}) collective-permute-start(bf16[448,32]{0,1:T(8,128)(2,1)S(1)} %get-tuple-element.74), channel_id=1, source_target_pairs={{0,2},{2,4},{4,6},{6,8},{8,10},{10,12},{12,14},{14,16},{16,18},{18... | collective-permute-start | bytes 86024
  561.4 37.6 %collective-permute-start.18 = (bf16[2432,32]{0,1:T(8,128)(2,1)S(1)}, bf16[2432,32]{0,1:T(8,128)(2,1)S(1)}, u32[]{:S(2)}, u32[]{:S(2)}) collective-permute-start(bf16[2432,32]{0,1:T(8,128)(2,1)S(1)} %copy-done.51), channel_id=1, source_target_pairs={{0,6},{2,8},{4,10},{6,12},{8,14},{10,16},{12,18},{14,20},{16,22},{... | collective-permute-start | bytes 466952
  567.4 31.7 %collective-permute-start.17 = (bf16[2432,32]{0,1:T(8,128)(2,1)S(1)}, bf16[2432,32]{0,1:T(8,128)(2,1)S(1)}, u32[]{:S(2)}, u32[]{:S(2)}) collective-permute-start(bf16[2432,32]{0,1:T(8,128)(2,1)S(1)} %copy-done.51), channel_id=1, source_target_pairs={{0,4},{2,6},{4,8},{6,10},{8,12},{10,14},{12,16},{14,18},{16,20},{1... | collective-permute-start | bytes 466952
  570.2 29.5 %collective-permute-start.16 = (bf16[2432,32]{0,1:T(8,128)(2,1)S(1)}, bf16[2432,32]{0,1:T(8,128)(2,1)S(1)}, u32[]{:S(2)}, u32[]{:S(2)}) collective-permute-start(bf16[2432,32]{0,1:T(8,128)(2,1)S(1)} %copy-done.51), channel_id=1, source_target_pairs={{0,2},{2,4},{4,6},{6,8},{8,10},{10,12},{12,14},{14,16},{16,18},{18... | collective-permute-start | bytes 466952
  572.9 26.1 %collective-permute-start.19 = (bf16[2432,28]{0,1:T(8,128)(2,1)S(1)}, bf16[2432,28]{0,1:T(8,128)(2,1)S(1)}, u32[]{:S(2)}, u32[]{:S(2)}) collective-permute-start(bf16[2432,28]{0,1:T(8,128)(2,1)S(1)} %slice.275), channel_id=1, source_target_pairs={{0,8},{2,10},{4,12},{6,14},{8,16},{10,18},{12,20},{14,22},{16,24},... | collective-permute-start | bytes 408584
  (186 other events, 2251.6 us)
Sparse Core Ops, SparseCore 0:
  309.1 415.2 all-reduce.11
where the time goes:
time: 746 us; the launch traced here: 733 us
  blocking collectives  234 us (31%)
  waiting for transfers between devices  131 us (18%)
  matrix products  115 us (15%)
  starting transfers between devices  114 us (15%)
  other arithmetic  61.3 us (8%)
  local copies, waits for them, and re-layouts  60 us (8%)
  between operations  18.8 us (3%)
    unnamed x1, blocking collectives  157 us
    unnamed x18, waiting for transfers between devices  128 us
    unnamed x17, starting transfers between devices  70.3 us
    all_to_all x10, blocking collectives, copy_for_each(): lax.all_to_all(jnp.broadcast_to(shard[None], (peers, *shard.shape)), axis...  40.5 us
    all_to_all x9, blocking collectives, sent_and_summed(): lax.all_to_all(tiles, axis, split_axis=0, concat_axis=0, tiled=True)  36.4 us
    convert_element_type x1, local copies, waits for them, and re-layouts, body(): totals[3].astype(jnp.bfloat16)  34.4 us
    dot_general x3, matrix products, backward(): jnp.einsum('id,igf->dgf', normed_two, grad_gate_up, preferred_element_typ...  33.2 us
    all_to_all x3, starting transfers between devices, copy_for_each(): lax.all_to_all(jnp.broadcast_to(shard[None], (peers, *shard.shape)), axis...  23.6 us
  transfers between devices with their start and end apart: 27, of which 5 were waited for; matrix products, arithmetic and copies ran while one was open for 33% of the time, Pallas kernels for 0%

commit v1 on v0

v1 whole, which is shorter than its diff:
```python
import functools

import jax
import jax.numpy as jnp
import numpy as np
from jax import lax
from jax.experimental import pallas as pl
from jax.experimental.pallas import tpu as pltpu
from jax.sharding import PartitionSpec as P

D = 896
HEADS = 14
HEAD = 64
CAP = 128
SEQS = 4
MICRO = 2
ROWS = MICRO * CAP
OWN = CAP // 2
FH = 2432
QW = 448
EPS = 1e-06
THETA = 1000000.0
MIB = 1024 * 1024

BF = jnp.bfloat16
F32 = jnp.float32
MESH = pl.DeviceIdType.MESH
VMEM = pltpu.VMEM

UP_A = 640
A_UP = FH
A_OUT = FH + UP_A
A_QKV = A_OUT + 512
HALF = A_QKV + 640
B_UP = FH
assert HALF == FH + FH - UP_A
TILES = ((0, 512), (512, 512), (1024, 512), (1536, 512), (2048, 384))
WIDE = ((0, 256), (256, 256), (512, 256), (768, 128))


def nn(a, b):
    return lax.dot_general(a, b, (((1,), (0,)), ((), ())), preferred_element_type=F32)


def nt(a, b):
    return lax.dot_general(a, b, (((1,), (1,)), ((), ())), preferred_element_type=F32)


def tn(a, b):
    return lax.dot_general(a, b, (((0,), (0,)), ((), ())), preferred_element_type=F32)


def rope_table():
    half = HEAD // 2
    frequency = np.power(np.float32(THETA), -(np.arange(half, dtype=np.float32) * np.float32(2.0 / HEAD)))
    phases = (np.arange(CAP, dtype=np.float32)[:, None] * frequency[None, :].astype(np.float32)).astype(np.float32)
    phases = phases.astype(np.float64)
    cosine = np.concatenate([np.cos(phases)] * 4, axis=1).astype(np.float32)
    sine = np.concatenate([-np.sin(phases), np.sin(phases)] * 2, axis=1).astype(np.float32)
    parts = []
    for table in (cosine, sine):
        rest = table
        for _ in range(3):
            piece = rest.astype(jnp.bfloat16)
            parts.append(piece)
            rest = rest - piece.astype(np.float32)
    return np.concatenate(parts, axis=1)


def row_orders():
    index = np.arange(D)
    first, second, x_hi, k = index // 224, index // 56 % 4, index // 28 % 2, index % 28
    orders = []
    for y, z in ((first, second), (second, first)):
        source = (x_hi * 16 + z * 4 + y) * 28 + k
        orders.append((source[:, None] == np.arange(D)[None, :]).astype(jnp.bfloat16))
    return np.stack(orders)


def turn(block, lane):
    low = (lane & 63) < 32
    return jnp.where(low, pltpu.roll(block, 96, 1), pltpu.roll(block, 32, 1))


def layer_kernel(
    len_ref, x_ref, cot_ref, g1_ref, g2_ref, b_ref, tab_ref,
    wq_hbm, wkv_hbm, wo_hbm, wgu_hbm, wd_hbm, perm_hbm,
    so_ref, ig_ref, ga_ref, gb_ref, small_ref,
    wqkv, wo, wgu, wd, perm, xbuf, gbuf, e1s, e1r, e2s, e2r, e3s, e3r, e4s, e4r, pipe_out,
    n1, n2, qb, kb, vb, pmat, mix, middle, gate, up, hidden, dgate, dup, lt, part, gmid, cs, allow,
    gqkv, load_sem, send_sem, recv_sem,
):
    pipe = lax.axis_index("pipe")
    t = lax.axis_index("tensor")
    other = 1 - t

    loads = [
        pltpu.make_async_copy(wq_hbm, wqkv.at[pl.ds(0, QW)], load_sem.at[0]),
        pltpu.make_async_copy(wkv_hbm, wqkv.at[pl.ds(QW, 128)], load_sem.at[1]),
        pltpu.make_async_copy(wo_hbm, wo.at[pl.ds(0, QW)], load_sem.at[2]),
        pltpu.make_async_copy(wgu_hbm, wgu, load_sem.at[3]),
        pltpu.make_async_copy(wd_hbm, wd, load_sem.at[4]),
        pltpu.make_async_copy(perm_hbm, perm, load_sem.at[5]),
    ]
    for c in loads:
        c.start()

    def to_core(src, dst, i):
        return pltpu.make_async_remote_copy(
            src_ref=src, dst_ref=dst, send_sem=send_sem.at[i], recv_sem=recv_sem.at[i],
            device_id={"tensor": other}, device_id_type=MESH)

    def to_pipe(src, dst, i):
        return pltpu.make_async_remote_copy(
            src_ref=src, dst_ref=dst, send_sem=send_sem.at[i], recv_sem=recv_sem.at[i],
            device_id={"pipe": 1 - pipe}, device_id_type=MESH)

    share_x = to_core(xbuf.at[:, t], xbuf.at[:, t], 0)
    share_g = to_core(gbuf.at[:, t], gbuf.at[:, t], 1)
    pass_x = to_pipe(so_ref, xbuf.at[:, t], 2)
    pass_g = to_pipe(pipe_out, gbuf.at[:, t], 3)
    swap_1 = to_core(e1s, e1r, 4)
    swap_2 = to_core(e2s, e2r, 5)
    swap_3 = to_core(e3s, e3r, 6)
    swap_4 = to_core(e4s, e4r, 7)

    barrier = pltpu.get_barrier_semaphore()
    pl.semaphore_signal(barrier, inc=1, device_id={"tensor": other}, device_id_type=MESH)
    pl.semaphore_signal(barrier, inc=1, device_id={"pipe": 1 - pipe}, device_id_type=MESH)
    pl.semaphore_wait(barrier, 2)

    @pl.when(pipe == 0)
    def _():
        xbuf[:, t] = x_ref[...]

    @pl.when(pipe == 1)
    def _():
        gbuf[:, t] = cot_ref[...]
        share_g.start()

    wqkv[pl.ds(QW + 128, 64), :] = jnp.zeros((64, D), BF)
    wo[pl.ds(QW, 64), :] = jnp.zeros((64, D), BF)
    slot = lax.broadcasted_iota(jnp.int32, (CAP, CAP), 0)
    lane = lax.broadcasted_iota(jnp.int32, (CAP, CAP), 1)
    for m in range(MICRO):
        end = 0
        seg_row = jnp.zeros((CAP, CAP), jnp.int32)
        seg_col = jnp.zeros((CAP, CAP), jnp.int32)
        start = jnp.zeros((CAP, CAP), jnp.int32)
        for s in range(SEQS):
            end = end + len_ref[m, s]
            passed = slot >= end
            seg_row = seg_row + passed.astype(jnp.int32)
            seg_col = seg_col + (lane >= end).astype(jnp.int32)
            start = jnp.where(passed, end, start)
        allow[m] = jnp.where((seg_row == seg_col) & (lane <= slot), 1.0, 0.0)
        cs[m, 2] = jnp.where((seg_row < SEQS) | (pipe == 0), 1.0, 0.0)
        one_hot = jnp.where(slot - start == lane, 1.0, 0.0).astype(BF)
        table = nn(one_hot, tab_ref[...])
        cs[m, 0] = table[:, :128] + table[:, 128:256] + table[:, 256:384]
        cs[m, 1] = table[:, 384:512] + table[:, 512:640] + table[:, 640:768]

    @pl.when(pipe == 1)
    def _():
        pass_x.wait_recv()

    share_x.start()
    share_x.wait()
    stream = xbuf[...].astype(F32).reshape(ROWS, D)
    inv = lax.rsqrt(jnp.mean(stream * stream, axis=-1, keepdims=True) + EPS)
    n1[...] = (stream * inv * g1_ref[...]).astype(BF)
    loads[0].wait()
    loads[1].wait()
    half_lane = lax.broadcasted_iota(jnp.int32, (CAP, 128), 1)
    for m in range(MICRO):
        rows = pl.ds(m * CAP, CAP)
        qkv = nt(n1[rows, :], wqkv[...]) + b_ref[...]
        for j in range(4):
            block = qkv[:, j * 128:(j + 1) * 128]
            block = block * cs[m, 0] + turn(block, half_lane) * cs[m, 1]
            qb[m, j] = block.astype(BF)
            if j == 3:
                odd = jnp.where(half_lane >= 64, block, 0.0)
                kb[m, 1] = odd.astype(BF)
                kb[m, 0] = pltpu.roll(odd, 64, 1).astype(BF)
        even = jnp.where(half_lane < 64, qkv[:, 512:640], 0.0)
        vb[m, 0] = even.astype(BF)
        vb[m, 1] = pltpu.roll(even, 64, 1).astype(BF)
    for m in range(MICRO):
        q_even = qb[m].reshape(4 * CAP, 128)
        q_odd = qb[m, :3].reshape(3 * CAP, 128)
        seen = allow[m] > 0.0
        mixed = []
        for parity, queries, count in ((0, q_even, 4), (1, q_odd, 3)):
            scores = nt(queries, kb[m, parity]).reshape(count, CAP, CAP) * HEAD ** (-0.5)
            scores = jnp.where(seen[None], scores, -1e30)
            top = jnp.max(scores, axis=-1, keepdims=True)
            grown = jnp.exp(scores - top)
            p = grown * (1.0 / jnp.sum(grown, axis=-1, keepdims=True))
            pmat[m, pl.ds(4 * parity, count)] = p
            mixed.append(nn(p.reshape(count * CAP, CAP).astype(BF), vb[m, parity]))
        for j in range(4):
            block = mixed[0][j * CAP:(j + 1) * CAP]
            if j < 3:
                block = block + mixed[1][j * CAP:(j + 1) * CAP]
            mix[pl.ds(m * CAP, CAP), j * 128:(j + 1) * 128] = block.astype(BF)
    loads[2].wait()
    for c, w in WIDE:
        e1s[:, c:c + w] = nn(mix[...], wo[:, c:c + w]).astype(BF)
    swap_1.start()
    swap_1.wait()
    mid = stream + (e1s[...].astype(F32) + e1r[...].astype(F32))
    middle[...] = mid.reshape(MICRO, 2, OWN, D)
    inv = lax.rsqrt(jnp.mean(mid * mid, axis=-1, keepdims=True) + EPS)
    n2[...] = (mid * inv * g2_ref[...]).astype(BF)
    loads[3].wait()
    for c, w in TILES:
        g = nn(n2[...], wgu[0, :, c:c + w])
        u = nn(n2[...], wgu[1, :, c:c + w])
        gate[:, c:c + w] = g
        up[:, c:c + w] = u
        hidden[:, c:c + w] = (g * jax.nn.sigmoid(g) * u).astype(BF)
    loads[4].wait()
    for c, w in WIDE:
        part[:, :, :, c:c + w] = nn(hidden[...], wd[:, c:c + w]).reshape(MICRO, 2, OWN, w)
    e2s[...] = part[:, other].astype(BF)
    swap_2.start()
    swap_2.wait()
    so_ref[...] = (middle[:, t] + (part[:, t] + e2r[...].astype(F32))).astype(BF)

    @pl.when(pipe == 0)
    def _():
        pass_x.start()
        pass_g.wait_recv()
        share_g.start()

    loads[5].wait()
    share_g.wait()
    for m in range(MICRO):
        live = cs[m, 2][:, :1].astype(BF).reshape(2, OWN, 1)
        gbuf[m] = gbuf[m] * live
    grad = gbuf[...].reshape(ROWS, D)

    def flip(which, rows):
        return nt(perm[which], rows).astype(BF)

    def put(ref, at, w, value):
        ref[:, :, at:at + w] = value.astype(BF).reshape(4, 224, w)

    lt[...] = flip(0, grad)
    for c, w in TILES:
        put(ga_ref, c, w, nn(lt[...], hidden[:, c:c + w]))
    for c, w in TILES:
        gh = nt(grad, wd[c:c + w, :])
        g = gate[:, c:c + w]
        sig = jax.nn.sigmoid(g)
        dgate[:, c:c + w] = (gh * up[:, c:c + w] * sig * (1.0 + g * (1.0 - sig))).astype(BF)
        dup[:, c:c + w] = (gh * g * sig).astype(BF)
    for c, w in WIDE:
        e3s[:, c:c + w] = (nt(dgate[...], wgu[0, c:c + w, :]) + nt(dup[...], wgu[1, c:c + w, :])).astype(BF)
    swap_3.start()
    lt[...] = flip(1, n2[...])
    for c, w in TILES:
        put(gb_ref, c, w, nn(lt[...], dgate[:, c:c + w]))
    for c, w in ((640, 512), (1152, 512), (1664, 512), (2176, 256)):
        put(gb_ref, B_UP + c - UP_A, w, nn(lt[...], dup[:, c:c + w]))
    lt[...] = flip(0, n2[...])
    put(ga_ref, A_UP, UP_A, nn(lt[...], dup[:, :UP_A]))
    swap_3.wait()

    def norm_back(grads, values, gain):
        inverse = lax.rsqrt(jnp.mean(values * values, axis=-1, keepdims=True) + EPS)
        scaled = values * inverse
        weighted = grads * gain
        back = inverse * (weighted - scaled * jnp.mean(weighted * scaled, axis=-1, keepdims=True))
        return back, grads * scaled

    grads = e3s[...].astype(F32) + e3r[...].astype(F32)
    back, terms = norm_back(grads, middle[...].reshape(ROWS, D), g2_ref[...])
    row = lax.broadcasted_iota(jnp.int32, (ROWS, 1), 0)
    mine = ((row >> 6) & 1) == t
    small_ref[...] = jnp.zeros((8, D), F32)
    small_ref[1:2, :] = jnp.sum(jnp.where(mine, terms, 0.0), axis=0, keepdims=True)
    grad_mid = grad.astype(F32) + back
    gmid[...] = grad_mid.reshape(MICRO, 2, OWN, D)
    mb = grad_mid.astype(BF)
    lt[...] = flip(0, mb)
    put(ga_ref, A_OUT, 512, nn(lt[...], mix[...]))
    gmix = nt(mb, wo[...]).astype(BF)
    for m in range(MICRO):
        blocks = [gmix[m * CAP:(m + 1) * CAP, j * 128:(j + 1) * 128] for j in range(4)]
        q_even = qb[m].reshape(4 * CAP, 128)
        q_odd = qb[m, :3].reshape(3 * CAP, 128)
        out = []
        for parity, queries, count in ((0, q_even, 4), (1, q_odd, 3)):
            gm = jnp.concatenate(blocks[:count], axis=0)
            p = pmat[m, pl.ds(4 * parity, count)].reshape(count * CAP, CAP)
            gp = nt(gm, vb[m, parity])
            ds = (p * (gp - jnp.sum(p * gp, axis=-1, keepdims=True))).astype(BF)
            out.append((nn(ds, kb[m, parity]), tn(ds, queries), tn(p.astype(BF), gm)))
        keys = pltpu.roll(out[0][1], 64, 1) + out[1][1]
        values = out[0][2] + pltpu.roll(out[1][2], 64, 1)
        rows = pl.ds(m * CAP, CAP)
        for j in range(4):
            block = out[0][0][j * CAP:(j + 1) * CAP]
            if j < 3:
                block = block + out[1][0][j * CAP:(j + 1) * CAP]
            else:
                block = jnp.where(half_lane < 64, block, keys)
            block = block * HEAD ** (-0.5)
            block = block * cs[m, 0] - turn(block, half_lane) * cs[m, 1]
            gqkv[rows, j * 128:(j + 1) * 128] = block.astype(BF)
        gqkv[rows, 512:640] = jnp.where(half_lane < 64, values, 0.0).astype(BF)
    for c, w in WIDE:
        part[:, :, :, c:c + w] = nn(gqkv[...], wqkv[:, c:c + w]).reshape(MICRO, 2, OWN, w)
    e4s[...] = part[:, other].astype(BF)
    swap_4.start()
    swap_4.wait()
    grads = (part[:, t] + e4r[...].astype(F32)).reshape(MICRO * OWN, D)
    back, terms = norm_back(grads, xbuf[:, t].astype(F32).reshape(MICRO * OWN, D), g1_ref[...])
    total = gmid[:, t] + back.reshape(MICRO, OWN, D)
    ig_ref[...] = total
    pipe_out[...] = total.astype(BF)

    @pl.when(pipe == 1)
    def _():
        pass_g.start()

    small_ref[0:1, :] = jnp.sum(terms, axis=0, keepdims=True)
    bias = jnp.sum(gqkv[...].astype(F32), axis=0, keepdims=True)
    for c in range(2):
        small_ref[2 + c:3 + c, :640] = jnp.where(t == c, bias, 0.0)
    lt[...] = flip(0, n1[...])
    put(ga_ref, A_QKV, 640, nn(lt[...], gqkv[...]))

    @pl.when(pipe == 0)
    def _():
        pass_x.wait_send()

    @pl.when(pipe == 1)
    def _():
        pass_g.wait_send()


def run_layers(lens, x, cot, g1, g2, bias, wq, wkv, wo, wgu, wd):
    vmem = pl.BlockSpec(memory_space=VMEM)
    hbm = pl.BlockSpec(memory_space=pl.ANY)
    return pl.pallas_call(
        layer_kernel,
        out_shape=(
            jax.ShapeDtypeStruct((MICRO, OWN, D), BF),
            jax.ShapeDtypeStruct((MICRO, OWN, D), F32),
            jax.ShapeDtypeStruct((4, 224, HALF), BF),
            jax.ShapeDtypeStruct((4, 224, HALF), BF),
            jax.ShapeDtypeStruct((8, D), F32),
        ),
        in_specs=[pl.BlockSpec(memory_space=pltpu.SMEM)] + [vmem] * 6 + [hbm] * 6,
        out_specs=(vmem,) * 5,
        scratch_shapes=[
            VMEM((640, D), BF), VMEM((512, D), BF), VMEM((2, D, FH), BF), VMEM((FH, D), BF), VMEM((2, D, D), BF),
            VMEM((MICRO, 2, OWN, D), BF), VMEM((MICRO, 2, OWN, D), BF),
            VMEM((ROWS, D), BF), VMEM((ROWS, D), BF),
            VMEM((MICRO, OWN, D), BF), VMEM((MICRO, OWN, D), BF),
            VMEM((ROWS, D), BF), VMEM((ROWS, D), BF),
            VMEM((MICRO, OWN, D), BF), VMEM((MICRO, OWN, D), BF), VMEM((MICRO, OWN, D), BF),
            VMEM((ROWS, D), BF), VMEM((ROWS, D), BF),
            VMEM((MICRO, 4, CAP, 128), BF), VMEM((MICRO, 2, CAP, 128), BF), VMEM((MICRO, 2, CAP, 128), BF),
            VMEM((MICRO, 7, CAP, CAP), F32), VMEM((ROWS, 512), BF), VMEM((MICRO, 2, OWN, D), F32),
            VMEM((ROWS, FH), F32), VMEM((ROWS, FH), F32), VMEM((ROWS, FH), BF), VMEM((ROWS, FH), BF), VMEM((ROWS, FH), BF),
            VMEM((D, ROWS), BF), VMEM((MICRO, 2, OWN, D), F32), VMEM((MICRO, 2, OWN, D), F32),
            VMEM((MICRO, 3, CAP, 128), F32), VMEM((MICRO, CAP, CAP), F32), VMEM((ROWS, 640), BF),
            pltpu.SemaphoreType.DMA((6,)), pltpu.SemaphoreType.DMA((8,)), pltpu.SemaphoreType.DMA((8,)),
        ],
        compiler_params=pltpu.CompilerParams(collective_id=0, has_side_effects=True, vmem_limit_bytes=60 * MIB),
        name="layers",
    )(lens, x, cot, g1, g2, bias, jnp.asarray(rope_table()), wq, wkv, wo, wgu, wd, jnp.asarray(row_orders()))


PIECES = ((0, 1408), (1408, 1408), (2816, 1408))


def sum_kernel(
    g0_hbm, g1_hbm, small_ref, o0_ref, o1_ref, so_ref,
    grads, r1, r2, h2, q1, q2, h3, q3, small_in, load_sem, send_sem, recv_sem, small_send, small_recv,
):
    rank = lax.axis_index("dp")
    t = lax.axis_index("tensor")
    x_hi, z, y = rank // 16, (rank // 4) % 4, rank % 4

    def at(yy, zz, xx):
        return {"dp": xx * 16 + zz * 4 + yy}

    def along(axis, step):
        if axis == 0:
            return at((y + step) % 4, z, x_hi)
        return at(y, (z + step) % 4, x_hi)

    x_peer = at(y, z, 1 - x_hi)
    pos = (y, z)
    loads = []
    for h, src in ((0, g0_hbm), (1, g1_hbm)):
        for i, (c, w) in enumerate(PIECES):
            loads.append(pltpu.make_async_copy(src.at[:, :, pl.ds(c, w)], grads.at[h, :, :, pl.ds(c, w)], load_sem.at[h, i]))
    for i in range(len(PIECES)):
        for h in range(2):
            loads[h * len(PIECES) + i].start()

    barrier = pltpu.get_barrier_semaphore()
    peers = [along(0, 1), along(0, 3), along(1, 1), along(1, 3), x_peer, {"tensor": 1 - t}]
    for peer in peers:
        pl.semaphore_signal(barrier, inc=1, device_id=peer, device_id_type=MESH)
    pl.semaphore_wait(barrier, len(peers))

    def remote(src, dst, peer, *sem):
        return pltpu.make_async_remote_copy(
            src_ref=src, dst_ref=dst, send_sem=send_sem.at[sem], recv_sem=recv_sem.at[sem],
            device_id=peer, device_id_type=MESH)

    copies = {}

    def ring_copies(h, i, stage):
        c, w = PIECES[i]
        cols = pl.ds(c, w)
        axis = h if stage == 0 else 1 - h
        f = pos[axis]
        ahead, behind = along(axis, 1), along(axis, 3)
        if stage == 0:
            n, src, first, last = 112, grads.at[h], r1.at[h], r2.at[h]
        else:
            n, src, first, last = 32, h2.at[h], q1.at[h], q2.at[h]
        top, low = pl.ds(0, n), pl.ds(n, n)
        base = 6 * stage
        cp = [
            remote(src.at[(f + 2) % 4, top, cols], first.at[0, :, cols], ahead, h, i, base),
            remote(src.at[(f + 2) % 4, low, cols], first.at[1, :, cols], behind, h, i, base + 1),
            remote(src.at[(f + 1) % 4, low, cols], last.at[0, 1, :, cols], ahead, h, i, base + 2),
            remote(src.at[(f + 3) % 4, top, cols], last.at[1, 0, :, cols], behind, h, i, base + 3),
            remote(first.at[0, :, cols], last.at[0, 0, :, cols], ahead, h, i, base + 4),
            remote(first.at[1, :, cols], last.at[1, 1, :, cols], behind, h, i, base + 5),
        ]
        return cp, f, src, first, last, n, cols

    def ring_begin(h, i, stage):
        cp = ring_copies(h, i, stage)[0]
        copies[h, i, stage] = cp
        for k in range(4):
            cp[k].start()

    def ring_middle(h, i, stage):
        cp, f, src, first, last, n, cols = ring_copies(h, i, stage)
        for k, (chunk, part) in enumerate((((f + 1) % 4, 0), ((f + 3) % 4, 1))):
            cp[k].wait_recv()
            own = src[chunk, part * n:(part + 1) * n, cols]
            first[k, :, cols] = (own.astype(F32) + first[k, :, cols].astype(F32)).astype(BF)
            cp[4 + k].start()

    def ring_total(h, i, stage):
        cp, f, src, first, last, n, cols = ring_copies(h, i, stage)
        for k in range(2, 6):
            cp[k].wait_recv()
        sums = []
        for part in range(2):
            own = src[f, part * n:(part + 1) * n, cols]
            sums.append(own.astype(F32) + last[0, part, :, cols].astype(F32) + last[1, part, :, cols].astype(F32))
        return sums

    def second_begin(h, i):
        c, w = PIECES[i]
        top, low = ring_total(h, i, 0)
        for k in range(4):
            src = (top, low)[k // 2][(k % 2) * 56:(k % 2 + 1) * 56]
            h2[h, k, :56, c:c + w] = src.astype(BF)
            h2[h, k, 56:, c:c + w] = jnp.zeros((8, w), BF)
        ring_begin(h, i, 1)

    def third(h, i):
        c, w = PIECES[i]
        return remote(h3.at[h, :, pl.ds(c, w)], q3.at[h, :, pl.ds(c, w)], x_peer, h, i, 12)

    def third_begin(h, i):
        c, w = PIECES[i]
        top, low = ring_total(h, i, 1)
        both = jnp.concatenate([top, low], axis=0)
        first, last = both[:32], both[28:60]
        upper = x_hi == 1
        h3[h, :, c:c + w] = jnp.where(upper, first, last).astype(BF)
        (o0_ref, o1_ref)[h][:, c:c + w] = jnp.where(upper, last, first)[:28]
        third(h, i).start()

    def third_end(h, i):
        c, w = PIECES[i]
        third(h, i).wait_recv()
        out = (o0_ref, o1_ref)[h]
        out[:, c:c + w] = out[:, c:c + w] + q3[h, :, c:c + w].astype(F32)[:28]

    small_peers = [
        along(0, 1 + 2 * (y % 2)), along(0, 3 - 2 * (y % 2)),
        along(1, 1 + 2 * (z % 2)), along(1, 3 - 2 * (z % 2)), x_peer, {"tensor": 1 - t},
    ]

    def small_copy(k):
        return pltpu.make_async_remote_copy(
            src_ref=small_in.at[0, k], dst_ref=small_in.at[1, k], send_sem=small_send.at[k], recv_sem=small_recv.at[k],
            device_id=small_peers[k], device_id_type=MESH)

    def small_step(k):
        if k > 0:
            small_copy(k - 1).wait_recv()
            total = small_in[0, k - 1] + small_in[1, k - 1]
        else:
            total = small_ref[...]
        if k < 6:
            small_in[0, k] = total
            small_copy(k).start()
        else:
            so_ref[...] = total

    def begin(i):
        for h in range(2):
            loads[h * len(PIECES) + i].wait()
            ring_begin(h, i, 0)

    def both(f, *a):
        for h in range(2):
            f(h, *a)

    small_step(0)
    begin(0)
    begin(1)
    both(ring_middle, 0, 0)
    small_step(1)
    begin(2)
    both(ring_middle, 1, 0)
    small_step(2)
    both(second_begin, 0)
    both(ring_middle, 2, 0)
    small_step(3)
    both(ring_middle, 0, 1)
    both(second_begin, 1)
    small_step(4)
    both(third_begin, 0)
    both(ring_middle, 1, 1)
    both(second_begin, 2)
    small_step(5)
    both(third_begin, 1)
    both(ring_middle, 2, 1)
    both(third_end, 0)
    both(third_end, 1)
    both(third_begin, 2)
    small_step(6)
    both(third_end, 2)
    for i in range(len(PIECES)):
        for h in range(2):
            for stage in range(2):
                for cp in ring_copies(h, i, stage)[0]:
                    cp.wait_send()
            third(h, i).wait_send()
    for k in range(6):
        small_copy(k).wait_send()


def run_sums(ga, gb, small):
    vmem = pl.BlockSpec(memory_space=VMEM)
    hbm = pl.BlockSpec(memory_space=pl.ANY)
    count = len(PIECES)
    return pl.pallas_call(
        sum_kernel,
        out_shape=(
            jax.ShapeDtypeStruct((28, HALF), F32), jax.ShapeDtypeStruct((28, HALF), F32),
            jax.ShapeDtypeStruct((8, D), F32),
        ),
        in_specs=[hbm, hbm, vmem],
        out_specs=(vmem,) * 3,
        scratch_shapes=[
            VMEM((2, 4, 224, HALF), BF), VMEM((2, 2, 112, HALF), BF), VMEM((2, 2, 2, 112, HALF), BF),
            VMEM((2, 4, 64, HALF), BF), VMEM((2, 2, 32, HALF), BF), VMEM((2, 2, 2, 32, HALF), BF),
            VMEM((2, 32, HALF), BF), VMEM((2, 32, HALF), BF), VMEM((2, 6, 8, D), F32),
            pltpu.SemaphoreType.DMA((2, count)), pltpu.SemaphoreType.DMA((2, count, 13)), pltpu.SemaphoreType.DMA((2, count, 13)),
            pltpu.SemaphoreType.DMA((6,)), pltpu.SemaphoreType.DMA((6,)),
        ],
        compiler_params=pltpu.CompilerParams(collective_id=1, has_side_effects=True, vmem_limit_bytes=56 * MIB),
        name="sums",
    )(ga, gb, small)


def body(
    inputs, cotangent, lengths, gain_attn, w_query, b_query, w_keyval, b_keyval, w_out, gain_mlp, w_gate_up, w_down,
):
    bias = jnp.concatenate([b_query[0], b_keyval[0, 0], jnp.zeros((64,), BF)]).astype(F32)[None]
    outs = run_layers(
        lengths[:, 0], inputs, cotangent, gain_attn.astype(F32), gain_mlp.astype(F32), bias,
        jnp.swapaxes(w_query[0], 0, 1), jnp.swapaxes(w_keyval[0, :, 0], 0, 1), w_out[0],
        jnp.swapaxes(w_gate_up[0], 0, 1), w_down[0],
    )
    section_out, input_grad, ga, gb, small = outs
    sa, sb, total = run_sums(ga, gb, small)
    g_up = jnp.concatenate([sa[:, A_UP:A_UP + UP_A], sb[:, B_UP:]], axis=1)
    g_gate_up = jnp.stack([sb[:, :FH], g_up], axis=1)
    g_query = sa[:, A_QKV:A_QKV + QW]
    g_keyval = sa[:, A_QKV + QW:A_QKV + QW + 128]
    return (
        section_out[None],
        input_grad[None],
        total[0:1],
        g_query[None],
        total[2:4, :QW].reshape(1, HEADS * HEAD),
        g_keyval[None, :, None, :],
        total[2:4, QW:QW + 128][None],
        jnp.swapaxes(sa[:, A_OUT:A_OUT + QW], 0, 1)[None],
        total[1:2],
        g_gate_up[None],
        jnp.swapaxes(sa[:, :FH], 0, 1)[None],
    )


def solution(mesh):
    placed = (
        P(None, ("dp", "tensor"), None),
        P(None, ("dp", "tensor"), None),
        P(None, "dp", None),
        P("pipe", None),
        P("pipe", None, "tensor"),
        P("pipe", "tensor"),
        P("pipe", None, "tensor", None),
        P("pipe", "tensor", None),
        P("pipe", "tensor", None),
        P("pipe", None),
        P("pipe", None, None, "tensor"),
        P("pipe", "tensor", None),
    )
    return jax.shard_map(
        body,
        mesh=mesh,
        in_specs=placed,
        out_specs=(
            P("pipe", None, ("dp", "tensor"), None),
            P("pipe", None, ("dp", "tensor"), None),
            P("pipe", None),
            P("pipe", "dp", "tensor"),
            P("pipe", None),
            P("pipe", "dp", "tensor", None),
            P("pipe", None, None),
            P("pipe", "tensor", "dp"),
            P("pipe", None),
            P("pipe", "dp", None, "tensor"),
            P("pipe", "tensor", "dp"),
        ),
        check_vma=False,
    )
```

time: 746 us -> 212 us (0.28); the launches traced: 733 us -> 211 us
  blocking collectives: 234 us -> 0 us
  Pallas kernels: 0 us -> 183 us
  waiting for transfers between devices: 131 us -> 0 us
  matrix products: 115 us -> 0 us
  starting transfers between devices: 114 us -> 0 us
  other arithmetic: 61.3 us -> 3.95 us
  local copies, waits for them, and re-layouts: 60 us -> 24.2 us
  between operations: 18.8 us -> 0.71 us
    pallas_call x0 -> x2, Pallas kernels: none -> 183 us  [the longest x1 97.6 us: run_sums(): pl.pallas_call(sum_kernel, out_shape=(jax.ShapeDtypeStruct((28, HALF), F3...]
    unnamed x1 -> x0, blocking collectives: 157 us -> none
    unnamed x18 -> x0, waiting for transfers between devices: 128 us -> none
    dot_general x66 -> x0, matrix products: 115 us -> none  [the longest x3 33.2 us: backward(): jnp.einsum('id,igf->dgf', normed_two, grad_gate_up, preferred_element_typ...]
    all_to_all x19 -> x0, blocking collectives: 76.9 us -> none  [the longest x10 40.5 us: copy_for_each(): lax.all_to_all(jnp.broadcast_to(shard[None], (peers, *shard.shape)), axis...]
    unnamed x17 -> x0, starting transfers between devices: 70.3 us -> none
    all_to_all x6 -> x0, starting transfers between devices: 34.5 us -> none  [the longest x3 23.6 us: copy_for_each(): lax.all_to_all(jnp.broadcast_to(shard[None], (peers, *shard.shape)), axis...]
    convert_element_type x1 -> x0, local copies, waits for them, and re-layouts: 34.4 us -> none  [body(): totals[3].astype(jnp.bfloat16)]
  transfers between devices with their start and end apart: 27 -> 0, of which waited for: 5 -> 0; matrix products, arithmetic and copies ran while one was open for 33% -> 0% of each run, Pallas kernels for 0% -> 0%
where the time goes in v1:
time: 212 us; the launch traced here: 211 us
  Pallas kernels  183 us (86%)
  local copies, waits for them, and re-layouts  24.2 us (11%)
  other arithmetic  3.95 us (2%)
    pallas_call x1, Pallas kernels, run_sums(): pl.pallas_call(sum_kernel, out_shape=(jax.ShapeDtypeStruct((28, HALF), F3...  97.6 us
    pallas_call x1, Pallas kernels, run_layers(): pl.pallas_call(layer_kernel, out_shape=(jax.ShapeDtypeStruct((MICRO, OWN,...  85 us
    unnamed x13, local copies, waits for them, and re-layouts  15.3 us

profile of v1, /device:TPU:0, one launch (start us, length us, event | category | flops | bytes accessed | tf_op | source)
XLA Modules:
  0.0 211.4 jit_solution(8796794972742463704)
XLA Ops:
  0.7 0.1 pad.6.clone
  0.7 1.4 fusion.b_ref
  2.1 1.3 convert_element_type.16.g1_ref
  3.3 1.3 convert_element_type.17.g2_ref
  4.6 1.8 copy.25
  6.4 7.9 %copy.33 = bf16[1,896,2,2432]{3,1,2,0:T(8,128)(2,1)} copy(bf16[1,896,2,2432]{3,2,1,0:T(2,128)(2,1)} %param.24) | data formatting | bytes 17432576 | tf_op args[10]
  14.3 85.0 %layers.1 = (bf16[2,64,896]{2,1,0:T(8,128)(2,1)}, f32[2,64,896]{2,1,0:T(8,128)}, bf16[4,224,4224]{2,1,0:T(8,128)(2,1)}, bf16[4,224,4224]{2,1,0:T(8,128)(2,1)}, f32[8,896]{1,0:T(8,128)}) custom-call(s32[2,4]{1,0:T(2,128)} %bitcast.44, bf16[2,64,896]{2,1,0:T(8,128)(2,1)} %x_ref.1, bf16[2,64,896]{2,1,0:T(8,128)(2,1)} %cot_ref.1, ...), custom_call_target="tpu_custom_call" | custom-call | tf_op jit(solution)/shard_map/layers/pallas_call | solution.py:348
  99.3 97.6 %sums.1 = (f32[28,4224]{1,0:T(8,128)}, f32[28,4224]{1,0:T(8,128)}, f32[8,896]{1,0:T(8,128)}) custom-call(bf16[4,224,4224]{2,1,0:T(8,128)(2,1)} %get-tuple-element.21.g0_hbm, bf16[4,224,4224]{2,1,0:T(8,128)(2,1)} %get-tuple-element.22.g1_hbm, f32[8,896]{1,0:T(8,128)} %get-tuple-element.23.small_ref), custom_call_target="tpu_custom_call" | custom-call | tf_op jit(solution)/shard_map/sums/pallas_call | solution.py:566
  196.9 1.3 slice_bitcast_fusion.5
  198.2 0.7 slice.35
  198.9 1.4 fusion.1
  200.3 0.7 reshape.60
  201.0 0.8 slice_bitcast_fusion.4
  201.8 0.6 copy.28
  202.5 0.9 slice.41
  203.3 0.9 slice_bitcast_fusion.2
  204.2 0.7 copy.29
  204.9 0.7 copy.27
  205.6 1.1 slice_bitcast_fusion
  206.7 1.0 slice.42
  207.7 1.0 copy.31
  208.7 1.2 copy.30
  209.9 0.7 copy.36
  210.6 0.8 copy.37
  (7 shorter events, 0.1 us)
Async XLA Ops:
  99.3 110.7 %copy-start.1 = (bf16[2,64,896]{2,1,0:T(8,128)(2,1)S(1)}, bf16[2,64,896]{2,1,0:T(8,128)(2,1)}, u32[]{:S(2)}) copy-start(bf16[2,64,896]{2,1,0:T(8,128)(2,1)} %get-tuple-element.19) | copy-start | bytes 688132
  99.3 111.3 %copy-start = (f32[2,64,896]{2,1,0:T(8,128)S(1)}, f32[2,64,896]{2,1,0:T(8,128)}, u32[]{:S(2)}) copy-start(f32[2,64,896]{2,1,0:T(8,128)} %get-tuple-element.20) | copy-start | bytes 1376260

commit v2 on v1

v2 whole, which is shorter than its diff:
```python
import functools

import jax
import jax.numpy as jnp
import numpy as np
from jax import lax
from jax.experimental import pallas as pl
from jax.experimental.pallas import tpu as pltpu
from jax.sharding import PartitionSpec as P

D = 896
HEADS = 14
HEAD = 64
CAP = 128
SEQS = 4
MICRO = 2
ROWS = MICRO * CAP
OWN = CAP // 2
FH = 2432
QW = 448
EPS = 1e-06
THETA = 1000000.0
MIB = 1024 * 1024

BF = jnp.bfloat16
F32 = jnp.float32
MESH = pl.DeviceIdType.MESH
VMEM = pltpu.VMEM

UP_A = 640
A_UP = FH
A_OUT = FH + UP_A
A_Q = A_OUT + 512
A_KV = A_Q + 512
HALF = A_KV + 128
B_UP = FH
assert HALF == FH + FH - UP_A
TILES = ((0, 512), (512, 512), (1024, 512), (1536, 512), (2048, 384))
UP_TILES = ((640, 512), (1152, 512), (1664, 512), (2176, 256))
WIDE = ((0, 256), (256, 256), (512, 256), (768, 128))
PIECES = (
    (("down", 0, 1280, 0), ("down", 1280, 1152, 1280), ("up", 0, 640, A_UP), ("rest", 0, 1152, A_OUT)),
    (("gate", 0, 1280, 0), ("gate", 1280, 1152, 1280), ("up", 640, 896, B_UP), ("up", 1536, 896, B_UP + 896)),
)
COUNT = 4


def nn(a, b):
    return lax.dot_general(a, b, (((1,), (0,)), ((), ())), preferred_element_type=F32)


def nt(a, b):
    return lax.dot_general(a, b, (((1,), (1,)), ((), ())), preferred_element_type=F32)


def tn(a, b):
    return lax.dot_general(a, b, (((0,), (0,)), ((), ())), preferred_element_type=F32)


def rope_table():
    half = HEAD // 2
    frequency = np.power(np.float32(THETA), -(np.arange(half, dtype=np.float32) * np.float32(2.0 / HEAD)))
    phases = (np.arange(CAP, dtype=np.float32)[:, None] * frequency[None, :].astype(np.float32)).astype(np.float32)
    phases = phases.astype(np.float64)
    cosine = np.concatenate([np.cos(phases)] * 4, axis=1).astype(np.float32)
    sine = np.concatenate([-np.sin(phases), np.sin(phases)] * 2, axis=1).astype(np.float32)
    parts = []
    for table in (cosine, sine):
        rest = table
        for _ in range(3):
            piece = rest.astype(jnp.bfloat16)
            parts.append(piece)
            rest = rest - piece.astype(np.float32)
    return np.concatenate(parts, axis=1)


def row_order():
    index = np.arange(D)
    y, z, x_hi, k = index // 224, index // 56 % 4, index // 28 % 2, index % 28
    source = (x_hi * 16 + z * 4 + y) * 28 + k
    return (source[:, None] == np.arange(D)[None, :]).astype(jnp.bfloat16)


def turn(block, lane):
    low = (lane & 63) < 32
    return jnp.where(low, pltpu.roll(block, 96, 1), pltpu.roll(block, 32, 1))


def train_kernel(
    len_ref, x_ref, cot_ref, g1_ref, g2_ref, bq_ref, bkv_ref, tab_ref,
    wq_hbm, wkv_hbm, wo_hbm, wgu_hbm, wd_hbm, perm_hbm,
    so_ref, ig_ref, o0_ref, o1_ref, total_ref,
    wq, wkv, wo, wgu, wd, perm, xbuf, gbuf, e1s, e1r, e2s, e2r, pipe_out,
    n1, n2, qb, kb, vb, pmat, mix, middle, dgate, dup, hidden, lt, part, gmid, cs, allow, gqkv,
    mb_ref, gdown, grest, r1, r2, h2, q1, q2, h3, q3, small_in,
    load_sem, send_sem, recv_sem, sum_send, sum_recv, small_send, small_recv,
):
    pipe = lax.axis_index("pipe")
    t = lax.axis_index("tensor")
    rank = lax.axis_index("dp")
    other = 1 - t
    x_hi, z, y = rank // 16, (rank // 4) % 4, rank % 4
    pos = (y, z)

    loads = [
        pltpu.make_async_copy(wq_hbm, wq.at[pl.ds(0, QW)], load_sem.at[0]),
        pltpu.make_async_copy(wkv_hbm, wkv, load_sem.at[1]),
        pltpu.make_async_copy(wo_hbm, wo.at[pl.ds(0, QW)], load_sem.at[2]),
        pltpu.make_async_copy(wgu_hbm, wgu, load_sem.at[3]),
        pltpu.make_async_copy(wd_hbm, wd, load_sem.at[4]),
        pltpu.make_async_copy(perm_hbm, perm, load_sem.at[5]),
    ]
    for c in loads:
        c.start()

    def to_core(src, dst, i):
        return pltpu.make_async_remote_copy(
            src_ref=src, dst_ref=dst, send_sem=send_sem.at[i], recv_sem=recv_sem.at[i],
            device_id={"tensor": other}, device_id_type=MESH)

    def to_pipe(src, dst, i):
        return pltpu.make_async_remote_copy(
            src_ref=src, dst_ref=dst, send_sem=send_sem.at[i], recv_sem=recv_sem.at[i],
            device_id={"pipe": 1 - pipe}, device_id_type=MESH)

    share_x = to_core(xbuf.at[:, t], xbuf.at[:, t], 0)
    share_g = to_core(gbuf.at[:, t], gbuf.at[:, t], 1)
    pass_x = to_pipe(so_ref, xbuf.at[:, t], 2)
    pass_g = to_pipe(pipe_out, gbuf.at[:, t], 3)
    swap_1 = to_core(e1s, e1r, 4)
    swap_2 = to_core(e2s, e2r, 5)
    swap_3 = to_core(e1s, e1r, 6)
    swap_4 = to_core(e2s, e2r, 7)

    def at(yy, zz, xx):
        return {"dp": xx * 16 + zz * 4 + yy}

    def along(axis, step):
        if axis == 0:
            return at((y + step) % 4, z, x_hi)
        return at(y, (z + step) % 4, x_hi)

    x_peer = at(y, z, 1 - x_hi)
    peers = [along(0, 1), along(0, 3), along(1, 1), along(1, 3), x_peer, {"tensor": other}, {"pipe": 1 - pipe}]
    barrier = pltpu.get_barrier_semaphore()
    for peer in peers:
        pl.semaphore_signal(barrier, inc=1, device_id=peer, device_id_type=MESH)
    pl.semaphore_wait(barrier, len(peers))

    def remote(src, dst, peer, *sem):
        return pltpu.make_async_remote_copy(
            src_ref=src, dst_ref=dst, send_sem=sum_send.at[sem], recv_sem=sum_recv.at[sem],
            device_id=peer, device_id_type=MESH)

    def source(h, i, stage, q, half):
        name, c, w, at_col = PIECES[h][i]
        if stage == 1:
            return h2.at[h, q, pl.ds(32 * half, 32), pl.ds(at_col, w)]
        rows, cols = pl.ds(pl.multiple_of(q * 224 + 112 * half, 16), 112), pl.ds(c, w)
        if name == "down":
            return gdown.at[rows, cols]
        if name == "rest":
            return grest.at[rows, cols]
        return wgu.at[("gate", "up").index(name), rows, cols]

    def landing(h, i, stage):
        _, _, w, at_col = PIECES[h][i]
        cols = pl.ds(at_col, w)
        first, last = (r1, r2) if stage == 0 else (q1, q2)
        return (lambda k: first.at[h, k, :, cols]), (lambda k, half: last.at[h, k, half, :, cols])

    def ring_copy(h, i, stage, k):
        axis = h if stage == 0 else 1 - h
        f = pos[axis]
        first, last = landing(h, i, stage)
        ahead, behind = along(axis, 1), along(axis, 3)
        src, dst, peer = (
            lambda: (source(h, i, stage, (f + 2) % 4, 0), first(0), ahead),
            lambda: (source(h, i, stage, (f + 2) % 4, 1), first(1), behind),
            lambda: (source(h, i, stage, (f + 1) % 4, 1), last(0, 1), ahead),
            lambda: (source(h, i, stage, (f + 3) % 4, 0), last(1, 0), behind),
            lambda: (first(0), last(0, 0), ahead),
            lambda: (first(1), last(1, 1), behind),
        )[k]()
        return remote(src, dst, peer, h, i, 6 * stage + k)

    def begin(h, i, stage=0):
        for k in range(4):
            ring_copy(h, i, stage, k).start()

    def middle_of(h, i, stage):
        f = pos[h if stage == 0 else 1 - h]
        first, _ = landing(h, i, stage)
        for k, q in enumerate(((f + 1) % 4, (f + 3) % 4)):
            ring_copy(h, i, stage, k).wait_recv()
            own = source(h, i, stage, q, k)[...]
            slot = first(k)
            slot[...] = (own.astype(F32) + slot[...].astype(F32)).astype(BF)
            ring_copy(h, i, stage, 4 + k).start()

    def ring_total(h, i, stage):
        f = pos[h if stage == 0 else 1 - h]
        for k in range(2, 6):
            ring_copy(h, i, stage, k).wait_recv()
        _, last = landing(h, i, stage)
        sums = []
        for half in range(2):
            own = source(h, i, stage, f, half)[...]
            sums.append(own.astype(F32) + last(0, half)[...].astype(F32) + last(1, half)[...].astype(F32))
        return sums

    def second(h, i):
        _, _, w, c = PIECES[h][i]
        sums = ring_total(h, i, 0)
        for k in range(4):
            block = sums[k // 2][(k % 2) * 56:(k % 2 + 1) * 56]
            block = jnp.concatenate([block, jnp.zeros((8, w), F32)], axis=0)
            h2[h, k, :, c:c + w] = block.astype(BF)
        begin(h, i, 1)

    def third_copy(h, i):
        _, _, w, c = PIECES[h][i]
        return remote(h3.at[h, :, pl.ds(c, w)], q3.at[h, :, pl.ds(c, w)], x_peer, h, i, 12)

    def third(h, i):
        _, _, w, c = PIECES[h][i]
        both = jnp.concatenate(ring_total(h, i, 1), axis=0)
        first, last = both[:32], both[28:60]
        upper = x_hi == 1
        h3[h, :, c:c + w] = jnp.where(upper, first, last).astype(BF)
        (o0_ref, o1_ref)[h][:, c:c + w] = jnp.where(upper, last, first)[:28]
        third_copy(h, i).start()

    def third_end(h, i):
        _, _, w, c = PIECES[h][i]
        third_copy(h, i).wait_recv()
        out = (o0_ref, o1_ref)[h]
        out[:, c:c + w] = out[:, c:c + w] + q3[h, :, c:c + w].astype(F32)[:28]

    small_peers = [
        along(0, 1 + 2 * (y % 2)), along(0, 3 - 2 * (y % 2)),
        along(1, 1 + 2 * (z % 2)), along(1, 3 - 2 * (z % 2)), x_peer, {"tensor": other},
    ]

    def small_copy(k):
        return pltpu.make_async_remote_copy(
            src_ref=small_in.at[0, k], dst_ref=small_in.at[1, k], send_sem=small_send.at[k], recv_sem=small_recv.at[k],
            device_id=small_peers[k], device_id_type=MESH)

    def small_step(k):
        if k > 0:
            small_copy(k - 1).wait_recv()
            total = small_in[0, k - 1] + small_in[1, k - 1]
            if k < 6:
                small_in[0, k] = total
            else:
                total_ref[...] = total
        if k < 6:
            small_copy(k).start()

    @pl.when(pipe == 0)
    def _():
        xbuf[:, t] = x_ref[...]

    @pl.when(pipe == 1)
    def _():
        gbuf[:, t] = cot_ref[...]
        share_g.start()

    wq[pl.ds(QW, 64), :] = jnp.zeros((64, D), BF)
    wo[pl.ds(QW, 64), :] = jnp.zeros((64, D), BF)
    slot = lax.broadcasted_iota(jnp.int32, (CAP, CAP), 0)
    lane = lax.broadcasted_iota(jnp.int32, (CAP, CAP), 1)
    for m in range(MICRO):
        end = 0
        seg_row = jnp.zeros((CAP, CAP), jnp.int32)
        seg_col = jnp.zeros((CAP, CAP), jnp.int32)
        start = jnp.zeros((CAP, CAP), jnp.int32)
        for s in range(SEQS):
            end = end + len_ref[m, s]
            passed = slot >= end
            seg_row = seg_row + passed.astype(jnp.int32)
            seg_col = seg_col + (lane >= end).astype(jnp.int32)
            start = jnp.where(passed, end, start)
        allow[m] = jnp.where((seg_row == seg_col) & (lane <= slot), 1.0, 0.0)
        cs[m, 2] = jnp.where((seg_row < SEQS) | (pipe == 0), 1.0, 0.0)
        one_hot = jnp.where(slot - start == lane, 1.0, 0.0).astype(BF)
        table = nn(one_hot, tab_ref[...])
        cs[m, 0] = table[:, :128] + table[:, 128:256] + table[:, 256:384]
        cs[m, 1] = table[:, 384:512] + table[:, 512:640] + table[:, 640:768]
    bias_q = jnp.concatenate([bq_ref[...].astype(F32), jnp.zeros((1, 64), F32)], axis=1)
    bias_kv = bkv_ref[...].astype(F32)
    gain_1 = g1_ref[...].astype(F32)
    gain_2 = g2_ref[...].astype(F32)

    @pl.when(pipe == 1)
    def _():
        pass_x.wait_recv()

    share_x.start()
    share_x.wait()
    stream = xbuf[...].astype(F32).reshape(ROWS, D)
    inv = lax.rsqrt(jnp.mean(stream * stream, axis=-1, keepdims=True) + EPS)
    n1[...] = (stream * inv * gain_1).astype(BF)
    loads[0].wait()
    loads[1].wait()
    half_lane = lax.broadcasted_iota(jnp.int32, (CAP, 128), 1)
    for m in range(MICRO):
        rows = pl.ds(m * CAP, CAP)
        qs = nt(n1[rows, :], wq[...]) + bias_q
        vk = pltpu.roll(nn(n1[rows, :], wkv[...]) + bias_kv, 64, 1)
        for j in range(4):
            block = qs[:, j * 128:(j + 1) * 128]
            if j == 3:
                block = jnp.where(half_lane < 64, block, vk)
            block = block * cs[m, 0] + turn(block, half_lane) * cs[m, 1]
            qb[m, j] = block.astype(BF)
            if j == 3:
                odd = jnp.where(half_lane >= 64, block, 0.0)
                kb[m, 1] = odd.astype(BF)
                kb[m, 0] = pltpu.roll(odd, 64, 1).astype(BF)
        even = jnp.where(half_lane < 64, vk, 0.0)
        vb[m, 0] = even.astype(BF)
        vb[m, 1] = pltpu.roll(even, 64, 1).astype(BF)
    for m in range(MICRO):
        q_even = qb[m].reshape(4 * CAP, 128)
        q_odd = qb[m, :3].reshape(3 * CAP, 128)
        seen = allow[m] > 0.0
        mixed = []
        for parity, queries, count in ((0, q_even, 4), (1, q_odd, 3)):
            scores = nt(queries, kb[m, parity]).reshape(count, CAP, CAP) * HEAD ** (-0.5)
            scores = jnp.where(seen[None], scores, -1e30)
            top = jnp.max(scores, axis=-1, keepdims=True)
            grown = jnp.exp(scores - top)
            p = grown * (1.0 / jnp.sum(grown, axis=-1, keepdims=True))
            pmat[m, pl.ds(4 * parity, count)] = p
            mixed.append(nn(p.reshape(count * CAP, CAP).astype(BF), vb[m, parity]))
        for j in range(4):
            block = mixed[0][j * CAP:(j + 1) * CAP]
            if j < 3:
                block = block + mixed[1][j * CAP:(j + 1) * CAP]
            mix[pl.ds(m * CAP, CAP), j * 128:(j + 1) * 128] = block.astype(BF)
    loads[2].wait()
    for c, w in WIDE:
        e1s[:, c:c + w] = nn(mix[...], wo[:, c:c + w]).astype(BF)
    swap_1.start()
    swap_1.wait()
    mid = stream + (e1s[...].astype(F32) + e1r[...].astype(F32))
    middle[...] = mid.reshape(MICRO, 2, OWN, D)
    inv = lax.rsqrt(jnp.mean(mid * mid, axis=-1, keepdims=True) + EPS)
    n2[...] = (mid * inv * gain_2).astype(BF)
    loads[3].wait()
    for c, w in TILES:
        g = nn(n2[...], wgu[0, :, c:c + w])
        u = nn(n2[...], wgu[1, :, c:c + w])
        sig = jax.nn.sigmoid(g)
        silu = g * sig
        hidden[:, c:c + w] = (silu * u).astype(BF)
        dup[:, c:c + w] = silu.astype(BF)
        dgate[:, c:c + w] = (u * sig * (1.0 + g * (1.0 - sig))).astype(BF)
    loads[4].wait()
    for c, w in WIDE:
        part[:, :, :, c:c + w] = nn(hidden[...], wd[:, c:c + w]).reshape(MICRO, 2, OWN, w)
    e2s[...] = part[:, other].astype(BF)
    swap_2.start()
    swap_2.wait()
    so_ref[...] = (middle[:, t] + (part[:, t] + e2r[...].astype(F32))).astype(BF)

    @pl.when(pipe == 0)
    def _():
        pass_x.start()
        pass_g.wait_recv()
        share_g.start()

    loads[5].wait()
    share_g.wait()
    for m in range(MICRO):
        live = cs[m, 2][:, :1].astype(BF).reshape(2, OWN, 1)
        gbuf[m] = gbuf[m] * live

    def weights_down():
        lt[0] = nt(perm[...], gbuf[...].reshape(ROWS, D)).astype(BF)
        for i, tiles in enumerate((((0, 512), (512, 768)), ((1280, 512), (1792, 640)))):
            for c, w in tiles:
                gdown[:, c:c + w] = nn(lt[0], hidden[:, c:c + w]).astype(BF)
            begin(0, i)

    def weights_gate_up():
        turned = nt(perm[...], n2[...])
        lt[0] = turned.astype(BF)
        lt[1] = jnp.concatenate(
            [turned[(4 * b + a) * 56:(4 * b + a + 1) * 56] for a in range(4) for b in range(4)], axis=0).astype(BF)
        for i, tiles in enumerate((((0, 512), (512, 768)), ((1280, 512), (1792, 640)))):
            for c, w in tiles:
                wgu[0, :, c:c + w] = nn(lt[1], dgate[:, c:c + w]).astype(BF)
            begin(1, i)
        wgu[1, :, :UP_A] = nn(lt[0], dup[:, :UP_A]).astype(BF)
        begin(0, 2)
        for i, c in ((2, 640), (3, 1536)):
            wgu[1, :, c:c + 896] = nn(lt[1], dup[:, c:c + 896]).astype(BF)
            begin(1, i)

    @pl.when(pipe == 0)
    def _():
        weights_down()

    grad = gbuf[...].reshape(ROWS, D)
    for c, w in TILES:
        gh = nt(grad, wd[c:c + w, :])
        dgate[:, c:c + w] = (gh * dgate[:, c:c + w].astype(F32)).astype(BF)
        dup[:, c:c + w] = (gh * dup[:, c:c + w].astype(F32)).astype(BF)
    for c, w in WIDE:
        e1s[:, c:c + w] = (nt(dgate[...], wgu[0, c:c + w, :]) + nt(dup[...], wgu[1, c:c + w, :])).astype(BF)
    swap_3.start()

    @pl.when(pipe == 0)
    def _():
        weights_gate_up()

    swap_3.wait()

    def norm_back(grads, values, gain):
        inverse = lax.rsqrt(jnp.mean(values * values, axis=-1, keepdims=True) + EPS)
        scaled = values * inverse
        weighted = grads * gain
        back = inverse * (weighted - scaled * jnp.mean(weighted * scaled, axis=-1, keepdims=True))
        return back, grads * scaled

    grads = e1s[...].astype(F32) + e1r[...].astype(F32)
    back, terms = norm_back(grads, middle[...].reshape(ROWS, D), gain_2)
    row = lax.broadcasted_iota(jnp.int32, (ROWS, 1), 0)
    mine = ((row >> 6) & 1) == t
    small_in[0, 0] = jnp.zeros((8, D), F32)
    small_in[0, 0, 1:2, :] = jnp.sum(jnp.where(mine, terms, 0.0), axis=0, keepdims=True)
    grad_mid = gbuf[...].reshape(ROWS, D).astype(F32) + back
    gmid[...] = grad_mid.reshape(MICRO, 2, OWN, D)
    mb_ref[...] = grad_mid.astype(BF)
    gmix = nt(mb_ref[...], wo[...]).astype(BF)
    for m in range(MICRO):
        blocks = [gmix[m * CAP:(m + 1) * CAP, j * 128:(j + 1) * 128] for j in range(4)]
        q_even = qb[m].reshape(4 * CAP, 128)
        q_odd = qb[m, :3].reshape(3 * CAP, 128)
        out = []
        for parity, queries, count in ((0, q_even, 4), (1, q_odd, 3)):
            gm = jnp.concatenate(blocks[:count], axis=0)
            p = pmat[m, pl.ds(4 * parity, count)].reshape(count * CAP, CAP)
            gp = nt(gm, vb[m, parity])
            ds = (p * (gp - jnp.sum(p * gp, axis=-1, keepdims=True))).astype(BF)
            out.append((nn(ds, kb[m, parity]), tn(ds, queries), tn(p.astype(BF), gm)))
        keys = pltpu.roll(out[0][1], 64, 1) + out[1][1]
        values = out[0][2] + pltpu.roll(out[1][2], 64, 1)
        rows = pl.ds(m * CAP, CAP)
        for j in range(4):
            block = out[0][0][j * CAP:(j + 1) * CAP]
            if j < 3:
                block = block + out[1][0][j * CAP:(j + 1) * CAP]
            else:
                block = jnp.where(half_lane < 64, block, keys)
            block = block * HEAD ** (-0.5)
            block = block * cs[m, 0] - turn(block, half_lane) * cs[m, 1]
            if j == 3:
                gqkv[rows, 512:640] = pltpu.roll(jnp.where(half_lane < 64, values, block), 64, 1).astype(BF)
                block = jnp.where(half_lane < 64, block, 0.0)
            gqkv[rows, j * 128:(j + 1) * 128] = block.astype(BF)
    for c, w in WIDE:
        part[:, :, :, c:c + w] = (
            nn(gqkv[:, :512], wq[:, c:c + w]) + nt(gqkv[:, 512:], wkv[c:c + w, :])).reshape(MICRO, 2, OWN, w)
    e2s[...] = part[:, other].astype(BF)
    swap_4.start()
    swap_4.wait()
    grads = (part[:, t] + e2r[...].astype(F32)).reshape(MICRO * OWN, D)
    back, terms = norm_back(grads, xbuf[:, t].astype(F32).reshape(MICRO * OWN, D), gain_1)
    total = gmid[:, t] + back.reshape(MICRO, OWN, D)
    ig_ref[...] = total
    pipe_out[...] = total.astype(BF)

    @pl.when(pipe == 1)
    def _():
        pass_g.start()

    @pl.when(pipe == 1)
    def _():
        weights_down()
        weights_gate_up()

    lt[0] = nt(perm[...], mb_ref[...]).astype(BF)
    lt[1] = nt(perm[...], n1[...]).astype(BF)
    grest[:, :512] = nn(lt[0], mix[...]).astype(BF)
    grest[:, 512:] = nn(lt[1], gqkv[...]).astype(BF)
    begin(0, 3)
    small_in[0, 0, 0:1, :] = jnp.sum(terms, axis=0, keepdims=True)
    bias = jnp.sum(gqkv[...].astype(F32), axis=0, keepdims=True)
    wide = jnp.concatenate([bias[:, :512], jnp.zeros((1, D - 512), F32)], axis=1)
    small_in[0, 0, 2:3, :] = jnp.where(t == 0, wide, pltpu.roll(wide, QW, 1))
    for c in range(2):
        small_in[0, 0, 3 + c:4 + c, :128] = jnp.where(t == c, bias[:, 512:], 0.0)

    def both(f, *a):
        for h in range(2):
            f(h, *a)

    small_step(0)
    both(middle_of, 0, 0)
    small_step(1)
    both(middle_of, 1, 0)
    small_step(2)
    both(middle_of, 2, 0)
    small_step(3)
    both(middle_of, 3, 0)
    small_step(4)
    both(second, 0)
    small_step(5)
    both(second, 1)
    small_step(6)
    both(middle_of, 0, 1)
    both(second, 2)
    both(middle_of, 1, 1)
    both(third, 0)
    both(second, 3)
    both(middle_of, 2, 1)
    both(third, 1)
    both(middle_of, 3, 1)
    both(third, 2)
    both(third_end, 0)
    both(third_end, 1)
    both(third, 3)
    both(third_end, 2)
    both(third_end, 3)
    for i in range(COUNT):
        for h in range(2):
            for stage in range(2):
                for k in range(6):
                    ring_copy(h, i, stage, k).wait_send()
            third_copy(h, i).wait_send()
    for k in range(6):
        small_copy(k).wait_send()

    @pl.when(pipe == 0)
    def _():
        pass_x.wait_send()

    @pl.when(pipe == 1)
    def _():
        pass_g.wait_send()


def run_train(lens, x, cot, g1, g2, bq, bkv, wq, wkv, wo, wgu, wd):
    vmem = pl.BlockSpec(memory_space=VMEM)
    hbm = pl.BlockSpec(memory_space=pl.ANY)
    dma = pltpu.SemaphoreType.DMA
    return pl.pallas_call(
        train_kernel,
        out_shape=(
            jax.ShapeDtypeStruct((MICRO, OWN, D), BF),
            jax.ShapeDtypeStruct((MICRO, OWN, D), F32),
            jax.ShapeDtypeStruct((28, HALF), F32),
            jax.ShapeDtypeStruct((28, HALF), F32),
            jax.ShapeDtypeStruct((8, D), F32),
        ),
        in_specs=[pl.BlockSpec(memory_space=pltpu.SMEM)] + [vmem] * 7 + [hbm] * 6,
        out_specs=(vmem,) * 5,
        scratch_shapes=[
            VMEM((512, D), BF), VMEM((D, 128), BF), VMEM((512, D), BF), VMEM((2, D, FH), BF), VMEM((FH, D), BF), VMEM((D, D), BF),
            VMEM((MICRO, 2, OWN, D), BF), VMEM((MICRO, 2, OWN, D), BF),
            VMEM((ROWS, D), BF), VMEM((ROWS, D), BF),
            VMEM((MICRO, OWN, D), BF), VMEM((MICRO, OWN, D), BF), VMEM((MICRO, OWN, D), BF),
            VMEM((ROWS, D), BF), VMEM((ROWS, D), BF),
            VMEM((MICRO, 4, CAP, 128), BF), VMEM((MICRO, 2, CAP, 128), BF), VMEM((MICRO, 2, CAP, 128), BF),
            VMEM((MICRO, 7, CAP, CAP), F32), VMEM((ROWS, 512), BF), VMEM((MICRO, 2, OWN, D), F32),
            VMEM((ROWS, FH), BF), VMEM((ROWS, FH), BF), VMEM((ROWS, FH), BF),
            VMEM((2, D, ROWS), BF), VMEM((MICRO, 2, OWN, D), F32), VMEM((MICRO, 2, OWN, D), F32),
            VMEM((MICRO, 3, CAP, 128), F32), VMEM((MICRO, CAP, CAP), F32), VMEM((ROWS, 640), BF),
            VMEM((ROWS, D), BF), VMEM((D, FH), BF), VMEM((D, 1152), BF),
            VMEM((2, 2, 112, HALF), BF), VMEM((2, 2, 2, 112, HALF), BF),
            VMEM((2, 4, 64, HALF), BF), VMEM((2, 2, 32, HALF), BF), VMEM((2, 2, 2, 32, HALF), BF),
            VMEM((2, 32, HALF), BF), VMEM((2, 32, HALF), BF), VMEM((2, 6, 8, D), F32),
            dma((6,)), dma((8,)), dma((8,)), dma((2, COUNT, 13)), dma((2, COUNT, 13)), dma((6,)), dma((6,)),
        ],
        compiler_params=pltpu.CompilerParams(collective_id=0, has_side_effects=True, vmem_limit_bytes=63 * MIB),
        name="train",
    )(lens, x, cot, g1, g2, bq, bkv, jnp.asarray(rope_table()), wq, wkv, wo, wgu, wd, jnp.asarray(row_order()))


def place_kernel(
    so_in, ig_in, sa_ref, sb_ref, small_ref,
    so_ref, ig_ref, gain1_ref, gq_ref, bq_ref, gkv_ref, bkv_ref, go_ref, gain2_ref, ggu_ref, gd_ref,
):
    so_ref[...] = so_in[...]
    ig_ref[...] = ig_in[...]
    gain1_ref[...] = small_ref[0:1, :]
    gain2_ref[...] = small_ref[1:2, :]
    bq_ref[...] = small_ref[2:3, :]
    bkv_ref[...] = small_ref[3:5, :128]
    gq_ref[:, 0, :] = sa_ref[:, A_Q:A_Q + QW]
    gkv_ref[:, 0, :] = sa_ref[:, A_KV:]
    go_ref[:, 0, :] = sa_ref[:, A_OUT:A_OUT + QW]
    gd_ref[:, 0, :] = sa_ref[:, :FH]
    ggu_ref[:, 0, :] = sb_ref[:, :FH]
    ggu_ref[:, 1, :UP_A] = sa_ref[:, A_UP:A_OUT]
    ggu_ref[:, 1, UP_A:] = sb_ref[:, B_UP:]


def run_place(*arrays):
    vmem = pl.BlockSpec(memory_space=VMEM)
    shapes = (
        (MICRO, OWN, D), (MICRO, OWN, D), (1, D), (28, 1, QW), (1, D), (28, 1, 128), (2, 128),
        (28, 1, QW), (1, D), (28, 2, FH), (28, 1, FH),
    )
    return pl.pallas_call(
        place_kernel,
        out_shape=tuple(jax.ShapeDtypeStruct(s, F32 if i else BF) for i, s in enumerate(shapes)),
        in_specs=[vmem] * 5,
        out_specs=(vmem,) * 11,
        compiler_params=pltpu.CompilerParams(vmem_limit_bytes=32 * MIB),
        name="place",
    )(*arrays)


def body(
    inputs, cotangent, lengths, gain_attn, w_query, b_query, w_keyval, b_keyval, w_out, gain_mlp, w_gate_up, w_down,
):
    outs = run_train(
        lengths[:, 0], inputs, cotangent, gain_attn, gain_mlp, b_query, b_keyval[0],
        jnp.swapaxes(w_query[0], 0, 1), w_keyval[0, :, 0], w_out[0],
        jnp.swapaxes(w_gate_up[0], 0, 1), w_down[0],
    )
    so, ig, gain1, gq, bq, gkv, bkv, go, gain2, ggu, gd = run_place(*outs)
    return (
        so[None], ig[None], gain1, jnp.swapaxes(gq, 0, 1), bq, gkv[None], bkv[None],
        jnp.transpose(go, (1, 2, 0)), gain2, ggu[None], jnp.transpose(gd, (1, 2, 0)),
    )


def solution(mesh):
    placed = (
        P(None, ("dp", "tensor"), None),
        P(None, ("dp", "tensor"), None),
        P(None, "dp", None),
        P("pipe", None),
        P("pipe", None, "tensor"),
        P("pipe", "tensor"),
        P("pipe", None, "tensor", None),
        P("pipe", "tensor", None),
        P("pipe", "tensor", None),
        P("pipe", None),
        P("pipe", None, None, "tensor"),
        P("pipe", "tensor", None),
    )
    return jax.shard_map(
        body,
        mesh=mesh,
        in_specs=placed,
        out_specs=(
            P("pipe", None, ("dp", "tensor"), None),
            P("pipe", None, ("dp", "tensor"), None),
            P("pipe", None),
            P("pipe", "dp", "tensor"),
            P("pipe", None),
            P("pipe", "dp", "tensor", None),
            P("pipe", None, None),
            P("pipe", "tensor", "dp"),
            P("pipe", None),
            P("pipe", "dp", None, "tensor"),
            P("pipe", "tensor", "dp"),
        ),
        check_vma=False,
    )
```

time: 212 us -> 176 us (0.83)
  Pallas kernels: 183 us -> 162 us
  local copies, waits for them, and re-layouts: 24.2 us -> 12.7 us
  other arithmetic: 3.95 us -> 0 us
    pallas_call x2, Pallas kernels: 183 us -> 162 us  [the longest x1 161 us: run_train(): pl.pallas_call(train_kernel, out_shape=(jax.ShapeDtypeStruct((MICRO, OWN,...]
    broadcast_in_dim x5 -> x0, local copies, waits for them, and re-layouts: 4.15 us -> none  [the longest x1 1.33 us: body(): total[2:4, QW:QW + 128][None]]
    slice x4 -> x0, local copies, waits for them, and re-layouts: 3.98 us -> none  [the longest x2 1.85 us: body(): g_up = jnp.concatenate([sa[:, A_UP:A_UP + UP_A], sb[:, B_UP:]], axis=1)]
    convert_element_type x3 -> x0, other arithmetic: 3.88 us -> none  [the longest x1 1.35 us: body(): jnp.concatenate([b_query[0], b_keyval[0, 0], jnp.zeros((64,), BF)])]
    unnamed x13 -> x11, local copies, waits for them, and re-layouts: 15.3 us -> 12.7 us
where the time goes in v2:
time: 176 us; the launch traced here: 175 us
  Pallas kernels  162 us (92%)
  local copies, waits for them, and re-layouts  12.7 us (7%)
    pallas_call x1, Pallas kernels, run_train(): pl.pallas_call(train_kernel, out_shape=(jax.ShapeDtypeStruct((MICRO, OWN,...  161 us
    unnamed x11, local copies, waits for them, and re-layouts  12.7 us

profile of v2, /device:TPU:0, one launch (start us, length us, event | category | flops | bytes accessed | tf_op | source)
XLA Modules:
  0.0 175.2 jit_solution(5935957125488354583)
XLA Ops:
  0.6 7.9 %copy.27 = bf16[1,896,2,2432]{3,1,2,0:T(8,128)(2,1)} copy(bf16[1,896,2,2432]{3,2,1,0:T(2,128)(2,1)} %param.24) | data formatting | bytes 17432576 | tf_op args[10]
  8.5 160.5 %train.1 = (bf16[2,64,896]{2,1,0:T(8,128)(2,1)}, f32[2,64,896]{2,1,0:T(8,128)}, f32[28,4224]{1,0:T(8,128)}, f32[28,4224]{1,0:T(8,128)}, f32[8,896]{1,0:T(8,128)}) custom-call(s32[2,4]{1,0:T(2,128)} %bitcast.26, bf16[2,64,896]{2,1,0:T(8,128)(2,1)} %x_ref.1, bf16[2,64,896]{2,1,0:T(8,128)(2,1)} %cot_ref.1, bf16[1,896]{1,0:T(2,128)(2,1)} %g1_ref.1, ...), custom_call_target="tpu_custom_call" | custom-call | tf_op jit(solution)/shard_map/train/pallas_call | solution.py:551
  169.1 0.0 copy-start
  169.1 1.0 copy-done
  170.1 0.0 copy-start.1
  170.1 1.0 copy-done.1
  171.2 0.0 copy-start.2
  171.2 1.0 copy-done.2
  172.2 0.0 copy-start.3
  172.2 0.9 copy-done.3
  173.1 0.0 copy-start.4
  173.1 0.7 copy-done.4
  173.9 1.3 place.1
Async XLA Ops:
  169.1 1.0 copy-start
  170.1 1.0 copy-start.1
  171.2 1.0 copy-start.2
  172.2 0.9 copy-start.3
  173.1 0.7 copy-start.4
